TPU v7x, 256 devices: a whole 4x4x8 slice. The times are simulated.
256 devices in a mesh: section: 2 (over x_hi), dp: 32 (over z, x_lo, core), tensor: 4 (over y).
Axes of the slice: x: 4 (x_hi: 2, x_lo: 2; x = x_hi * 2 + x_lo), y: 4, z: 8, core: 2. Of those that a mesh axis runs over, the one named last changes fastest.
Arguments:
- left: bfloat16 [2, 16384, 8192], P('section', 'dp', 'tensor'), may hold values from -6 to 6
- weight: bfloat16 [2, 8192, 5120], P('section', ('tensor', 'dp')), may hold values from -0.0625 to 0.0625
- base: bfloat16 [2, 16384, 5120], P('section', 'dp', 'tensor'), may hold values from -6 to 6
- expo: int32 [2, 128, 40], P('section', 'dp', 'tensor'), may hold values from -7 to 2
- perm: int32 [2, 32, 4], P('section', 'dp'), may hold values from 0 to 3, each once within a row
Outputs:
- received: float32 [2, 16384, 5120], P('section', ('dp', 'tensor'))
Inputs may be any that keep to these rules, and one draw needn't show every extreme that they name: Each row of perm holds every number from 0 to 3 once.
All inputs are finite; a program needn't handle non-finite values.
Results may differ from a plain program's by a relative error of at most 0.01.
Values may be sent and summed in bfloat16 or wider, within the bound.
No kernel may reach another device: no remote copies, remote signals or barrier semaphores. Data moves between devices by JAX's collectives and lax.ppermute only.
A program may use at most 128 MiB of HBM per device.

v0:
```python
import functools
import math

import jax
import jax.numpy as jnp
import numpy as np
from jax import lax
from jax.experimental import pallas as pl
from jax.experimental.pallas import tpu as pltpu
from jax.sharding import PartitionSpec as P

TILE = 128
N_T = 4
N_Z = 8
GROUP = 4
DP = N_Z * GROUP
WIDE = 640
DEPTH = 2048
FULL = 5120
ROOT = 1.0 / math.sqrt(TILE)
MORE = 16
BOTH = 2 * WIDE
VMEM_LIMIT = 20 * 1024 * 1024
MIB = 1024 * 1024


def signs():
    index = np.arange(TILE)
    common = index[:, None] & index[None, :]
    parity = np.zeros((TILE, TILE), np.int64)
    for shift in range(7):
        parity += (common >> shift) & 1
    return jnp.asarray(1 - 2 * (parity & 1), jnp.bfloat16)


def call(body, out_shape, n_scalar, in_specs, out_specs, grid=(1,), scratch=(), cost=None, vmem=VMEM_LIMIT):
    return pl.pallas_call(
        body,
        out_shape=out_shape,
        grid_spec=pltpu.PrefetchScalarGridSpec(
            num_scalar_prefetch=n_scalar,
            grid=grid,
            in_specs=in_specs,
            out_specs=out_specs,
            scratch_shapes=scratch,
        ),
        compiler_params=pltpu.CompilerParams(vmem_limit_bytes=vmem),
        cost_estimate=cost,
    )


def local(body, out_shape, n_in, smem=0, scratch=(), cost=None):
    vmem = pl.BlockSpec(memory_space=pltpu.VMEM)
    scalar = pl.BlockSpec(memory_space=pltpu.SMEM)
    return pl.pallas_call(
        body,
        out_shape=out_shape,
        in_specs=[scalar] * smem + [vmem] * n_in,
        out_specs=[vmem] * len(out_shape) if isinstance(out_shape, list) else vmem,
        scratch_shapes=scratch,
        compiler_params=pltpu.CompilerParams(vmem_limit_bytes=VMEM_LIMIT),
        cost_estimate=cost,
    )


def cost_of(flops, moved):
    return pl.CostEstimate(flops=flops // 64, bytes_accessed=moved // 64, transcendentals=0)


def bf16(*shape):
    return jax.ShapeDtypeStruct(shape, jnp.bfloat16)


def copy_all(copies, sems):
    started = [pltpu.make_async_copy(src, dst, sems.at[i]) for i, (src, dst) in enumerate(copies)]
    for copy in started:
        copy.start()
    for copy in started:
        copy.wait()


def moving(body, out_shape, n_in, n_copies, cost):
    return pl.pallas_call(
        body,
        out_shape=out_shape,
        in_specs=[pl.BlockSpec(memory_space=pltpu.SMEM)] + [pl.BlockSpec(memory_space=pl.ANY)] * n_in,
        out_specs=jax.tree.map(lambda _: pl.BlockSpec(memory_space=pltpu.VMEM), out_shape),
        scratch_shapes=[pltpu.SemaphoreType.DMA((n_copies,))],
        compiler_params=pltpu.CompilerParams(vmem_limit_bytes=VMEM_LIMIT),
        cost_estimate=cost,
    )


def split_weight_body(sc, w_ref, *refs):
    copies = []
    for p, out in enumerate(refs[:GROUP]):
        for u in range(2):
            start = ((2 * (sc[2] ^ (p & 1)) + u) * 2 + (sc[1] ^ (p >> 1))) * WIDE
            part = w_ref.at[:, pl.ds(pl.multiple_of(start, TILE), WIDE)]
            copies.append((part, out.at[:, pl.ds(u * WIDE, WIDE)]))
    copy_all(copies, refs[GROUP])


def split_weight(sc, weight):
    rows = weight.shape[0]
    return moving(split_weight_body, [bf16(rows, BOTH)] * GROUP, 1, 2 * GROUP, cost_of(0, 4 * rows * FULL))(
        sc, weight
    )


def join_weight_body(sc, *refs):
    rows = refs[0].shape[0]
    for p in range(GROUP):
        start = pl.multiple_of((sc[2] ^ (p & 1)) * rows, rows)
        refs[GROUP + (p >> 1)][pl.ds(start, rows), :] = refs[p][...]


def join_weight(sc, pieces):
    rows = pieces[0].shape[0]
    return local(
        join_weight_body, [bf16(2 * rows, BOTH)] * 2, GROUP, smem=1, cost=cost_of(0, 16 * rows * BOTH)
    )(sc, *pieces)


def order_left_body(sc, left_ref, base_ref, near, far, sems):
    copies = []
    for k in range(N_T):
        j = sum(jnp.where(sc[4 + i] == sc[0] ^ k, i, 0) for i in range(N_T))
        rows = pl.ds(pl.multiple_of(j * TILE, TILE), TILE)
        for out, half in ((far, 1 - sc[1]), (near, sc[1])):
            cols = pl.ds(pl.multiple_of(half * WIDE, TILE), WIDE)
            copies.append((left_ref.at[rows, :], out.at[k, :, pl.ds(0, DEPTH)]))
            copies.append((base_ref.at[rows, cols], out.at[k, :, pl.ds(DEPTH, WIDE)]))
    copy_all(copies, sems)


def order_left(sc, left, base):
    out = bf16(N_T, TILE, DEPTH + WIDE)
    return moving(order_left_body, [out, out], 2, 4 * N_T, cost_of(0, 6 * MIB))(sc, left, base)


KEEP = ((0, 3), (0, 1))
GIVE = ((1, 2), (3, 2))
STEPS = ((1, 3), (3, 1))
PLAIN = 2


def product_body(kind, first, sc, *refs):
    if first:
        top, left, blocks, w, outs = refs[0], refs[1], refs[2 : 2 + 2 * N_Z], refs[-1], refs[2 + 2 * N_Z : -1]
        rows = DEPTH // N_Z // 2
        for j in range(N_Z):
            for side in range(2):
                z = (sc[3] + j) % N_Z
                start = pl.multiple_of((2 * z + (sc[1] ^ side)) * rows, rows)
                w[pl.ds(start, rows), :] = blocks[2 * j + side][...]
    else:
        left, w, outs = refs[0], refs[1], refs[2:]
    if kind == PLAIN:
        pairs = ((0, 1), (2, 3))
        places = [(outs[0].at[...], outs[1].at[...]), (outs[2].at[...], outs[3].at[...])]
    else:
        pairs = (KEEP[kind], GIVE[kind])
        places = [(out.at[0], out.at[1]) for out in outs]
    for pair, place in zip(pairs, places):
        a = jnp.concatenate([left[k, :, :DEPTH] for k in pair], axis=0)
        b = jnp.concatenate([left[k, :, DEPTH:] for k in pair], axis=0).astype(jnp.float32)
        for u in range(2):
            cols = slice(u * WIDE, (u + 1) * WIDE)
            mine = jnp.where((sc[0] == 2 * sc[2] + u), 1.0, 0.0)
            total = jnp.dot(a, w[:, cols], preferred_element_type=jnp.float32)
            total = (total + b * mine).astype(jnp.bfloat16)
            for i, out in enumerate(place):
                out[:TILE, cols] = total[i * TILE : (i + 1) * TILE]
        if first:
            for k, out in zip(pair, place):
                out[TILE:, :] = top[k]


PRODUCT_COST = cost_of(2 * N_T * TILE * DEPTH * BOTH, 8 * MIB)


def first_product(sc, kind, top, left, blocks):
    outs = local(
        functools.partial(product_body, kind, True),
        [bf16(TILE + MORE, BOTH)] * N_T + [bf16(DEPTH, BOTH)],
        2 + len(blocks),
        smem=1,
        cost=PRODUCT_COST,
    )(sc, top, left, *blocks)
    return outs[:N_T], outs[N_T]


def product(sc, kind, left, weight):
    return local(
        functools.partial(product_body, kind, False),
        [bf16(2, TILE, BOTH)] * 2,
        2,
        smem=1,
        cost=PRODUCT_COST,
    )(sc, left, weight)


def add_body(a_ref, b_ref, stay, leave):
    for i, out in enumerate((stay, leave)):
        out[...] = (a_ref[i].astype(jnp.float32) + b_ref[i].astype(jnp.float32)).astype(jnp.bfloat16)


def add(a, b):
    return local(add_body, [bf16(*a.shape[1:])] * 2, 2, cost=cost_of(a.size, 6 * a.size))(a, b)


def turn_body(h_ref, *refs):
    parts, out = refs[:-1], refs[-1]
    for j in range(BOTH // TILE):
        cols = slice(j * TILE, (j + 1) * TILE)
        total = jnp.dot(parts[0][:TILE, cols], h_ref[...], preferred_element_type=jnp.float32)
        for part in parts[1:]:
            total += jnp.dot(part[:TILE, cols], h_ref[...], preferred_element_type=jnp.float32)
        out[:TILE, cols] = (total * ROOT).astype(jnp.bfloat16)
    if out.shape[0] > TILE:
        total = parts[0][TILE:, :].astype(jnp.float32)
        for part in parts[1:]:
            total += part[TILE:, :].astype(jnp.float32)
        out[TILE:, :] = total.astype(jnp.bfloat16)


def turn(table, *parts):
    return local(
        turn_body, bf16(*parts[0].shape), 1 + len(parts), cost=cost_of(4 * TILE * TILE * BOTH, MIB)
    )(table, *parts)


def finish_body(sc, h_ref, *refs):
    pieces, out, lim = refs[:GROUP], refs[GROUP], refs[GROUP + 1]
    lim[...] = pieces[0][TILE:, :].astype(jnp.float32)
    for p, piece in enumerate(pieces):
        half = sc[1] ^ (p >> 1)
        for u in range(2):
            tensor = 2 * (sc[2] ^ (p & 1)) + u
            k = sc[0] ^ tensor
            top = lim[pl.ds(k, 1), pl.ds(pl.multiple_of(half * WIDE, TILE), WIDE)]
            first = tensor * 10 + half * (WIDE // TILE)
            for j in range(WIDE // TILE):
                limit = top[:, j * TILE : (j + 1) * TILE]
                value = piece[:TILE, u * WIDE + j * TILE : u * WIDE + (j + 1) * TILE].astype(jnp.float32)
                value = jnp.clip(value, -limit, limit).astype(jnp.bfloat16)
                value = jnp.dot(value, h_ref[...], preferred_element_type=jnp.float32)
                out[:, pl.ds(pl.multiple_of((first + j) * TILE, TILE), TILE)] = value * ROOT


def finish(sc, table, pieces):
    return local(
        finish_body,
        jax.ShapeDtypeStruct((TILE, FULL), jnp.float32),
        1 + GROUP,
        smem=1,
        scratch=[pltpu.VMEM((MORE, BOTH), jnp.float32)],
        cost=cost_of(2 * TILE * TILE * FULL, 4 * MIB),
    )(sc, table, *pieces)


def swap(value, offset):
    return lax.ppermute(value, "dp", [(i, i ^ offset) for i in range(DP)])


def cross(value, offset):
    pairs = [(s * DP + i, (1 - s) * DP + (i ^ offset)) for s in range(2) for i in range(DP)]
    return lax.ppermute(value, ("section", "dp"), pairs)


def along_y(value, offset):
    return lax.ppermute(value, "tensor", [(i, i ^ offset) for i in range(N_T)])


def along_z(value, steps):
    return lax.ppermute(value, "dp", [(i, (i + steps * GROUP) % DP) for i in range(DP)])


def after(value, *others):
    return lax.optimization_barrier((value, *others))[0]


def limits(expo, perm):
    here = lax.axis_index("tensor")
    top = 448.0 * jnp.exp2(expo.astype(jnp.float32))
    wanted = here ^ jnp.arange(N_T, dtype=jnp.int32)
    hit = perm[None, :] == wanted[:, None]
    top = jnp.sum(jnp.where(hit[:, :, None], top[None], 0.0), axis=1)
    place = jnp.arange(N_T)[:, None] == jnp.arange(MORE)[None, :]
    rows = jnp.where(place[..., None], top[:, None, :], 0.0)
    return jnp.repeat(rows, TILE, axis=2).astype(jnp.bfloat16)


def chain(values, *others):
    n = len(values)
    return lax.optimization_barrier((*values, *others))[:n]


def shards(left, weight, base, expo, perm):
    table = signs()
    dp = lax.axis_index("dp")
    sc = jnp.concatenate(
        [
            jnp.stack([lax.axis_index("tensor"), (dp // 2) % 2, dp % 2, dp // GROUP]).astype(jnp.int32),
            perm[0, 0],
        ]
    )
    pieces = split_weight(sc, weight[0])
    swapped = [None] + [swap(pieces[p], p) for p in range(1, GROUP)]
    top = limits(expo[0], perm[0, 0])

    near, far = order_left(sc, left[0], base[0])
    near_c = swap(near, 1)

    held = [{0: b} for b in join_weight(sc, [pieces[0], *chain(swapped[1:], near, top)])]
    far_x = swap(after(far, held[1][0]), 2)
    for s in range(1, 4):
        for h in held:
            h[N_Z - s], h[s] = along_z(h[(N_Z - s + 1) % N_Z], 1), along_z(h[s - 1], -1)
    held[0][4] = along_z(held[0][5], 1)
    held[1][4] = along_z(held[1][3], -1)

    def begin(parts, kind):
        return parts[0], along_y(parts[1], STEPS[kind][0]), kind

    def middle(begun, *wait):
        keep, got, kind = begun
        (got,) = chain((got,), *wait)
        stay, leave = add(keep, got)
        return stay, along_y(leave, STEPS[kind][1]), leave

    def end(middled, *wait):
        stay, got, _ = middled
        (got,) = chain((got,), *wait)
        return turn(table, stay, got)

    own, w = first_product(sc, PLAIN, top, near, [held[side][j] for j in range(N_Z) for side in range(2)])
    own_got = [along_y(own[k], k) for k in (2, 1, 3)]
    other = begin(product(sc, 0, near_c, w), 0)
    far_x = after(far_x, own[0])
    far_xc = swap(far_x, 1)
    across = begin(product(sc, 1, after(far_x, other[0]), w), 1)
    last = begin(product(sc, 0, after(far_xc, across[0]), w), 0)
    own_t = turn(table, own[0], *chain(own_got, last[0]))
    own_x = cross(own_t, 0)
    other = middle(other, own_t)
    across = middle(across, other[2])
    other_t = end(other, across[2], own_x)
    other_x = cross(other_t, 1)
    across_t = end(across, other_t)
    across_x = cross(across_t, 2)
    last = middle(last, across[2])
    last_t = end(last, across_t, other_x)
    last_x = cross(last_t, 3)
    return finish(sc, table, (own_x, other_x, across_x, last_x))[None]


def solution(mesh):
    in_specs = (
        P("section", "dp", "tensor"),
        P("section", ("tensor", "dp"), None),
        P("section", "dp", "tensor"),
        P("section", "dp", "tensor"),
        P("section", "dp", None),
    )
    out_specs = P("section", ("dp", "tensor"), None)
    return jax.shard_map(shards, mesh=mesh, in_specs=in_specs, out_specs=out_specs, check_vma=False)
```

profile of v0, /device:TPU:1, one launch (start us, length us, event | category | flops | bytes accessed | tf_op | source)
XLA Modules:
  0.0 152.1 jit_solution(532604333110697387)
XLA Ops:
  2.6 3.3 %collective-permute-start = (bf16[64,1280]{1,0:T(8,128)(2,1)S(1)}, bf16[64,1280]{1,0:T(8,128)(2,1)S(1)}, u32[]{:S(2)}, u32[]{:S(2)}) collective-permute-start(bf16[64,1280]{1,0:T(8,128)(2,1)S(1)} %get-tuple-element.48), channel_id=1, source_target_pairs={{0,4},{4,0},{8,12},{12,8},{16,20},{20,16},{24,28},{28,24},{32,36},... | collective-permute-start | bytes 491528 | tf_op jit(solution)/shard_map/ppermute | solution.py:264
  17.2 3.9 %collective-permute-start.4 = (bf16[128,1280]{1,0:T(8,128)(2,1)S(1)}, bf16[128,1280]{1,0:T(8,128)(2,1)S(1)}, u32[]{:S(2)}, u32[]{:S(2)}) collective-permute-start(bf16[128,1280]{1,0:T(8,128)(2,1)S(1)} %get-tuple-element.55.refs_3_), channel_id=1, source_target_pairs={{0,112},{4,116},{8,120},{12,124},{16,0},{20,4},{24,8},{28,12},{32,... | collective-permute-start | bytes 983048 | tf_op jit(solution)/shard_map/ppermute | solution.py:277
  23.8 5.0 %collective-permute-done.9.refs_16_ = bf16[128,1280]{1,0:T(8,128)(2,1)S(1)} collective-permute-done((bf16[128,1280]{1,0:T(8,128)(2,1)S(1)}, bf16[128,1280]{1,0:T(8,128)(2,1)S(1)}, u32[]{:S(2)}, u32[]{:S(2)}) %collective-permute-start.9) | collective-permute-done | bytes 327712 | tf_op jit(solution)/shard_map/ppermute | solution.py:277
  28.7 2.7 %collective-permute-start.6 = (bf16[128,1280]{1,0:T(8,128)(2,1)S(1)}, bf16[128,1280]{1,0:T(8,128)(2,1)S(1)}, u32[]{:S(2)}, u32[]{:S(2)}) collective-permute-start(bf16[128,1280]{1,0:T(8,128)(2,1)S(1)} %collective-permute-done.4.refs_5_), channel_id=1, source_target_pairs={{0,112},{4,116},{8,120},{12,124},{16,0},{20,4},{24,8},{28,12},{32,... | collective-permute-start | bytes 983048 | tf_op jit(solution)/shard_map/ppermute | solution.py:277
  31.4 4.3 %collective-permute-done.14.refs_17_ = bf16[128,1280]{1,0:T(8,128)(2,1)S(1)} collective-permute-done((bf16[128,1280]{1,0:T(8,128)(2,1)S(1)}, bf16[128,1280]{1,0:T(8,128)(2,1)S(1)}, u32[]{:S(2)}, u32[]{:S(2)}) %collective-permute-start.14) | collective-permute-done | bytes 327712 | tf_op jit(solution)/shard_map/ppermute | solution.py:277
  35.8 2.7 %collective-permute-start.5 = (bf16[128,1280]{1,0:T(8,128)(2,1)S(1)}, bf16[128,1280]{1,0:T(8,128)(2,1)S(1)}, u32[]{:S(2)}, u32[]{:S(2)}) collective-permute-start(bf16[128,1280]{1,0:T(8,128)(2,1)S(1)} %collective-permute-done.3.refs_4_), channel_id=1, source_target_pairs={{0,112},{4,116},{8,120},{12,124},{16,0},{20,4},{24,8},{28,12},{32,... | collective-permute-start | bytes 983048 | tf_op jit(solution)/shard_map/ppermute | solution.py:277
  38.4 4.3 %collective-permute-done.10.refs_14_ = bf16[128,1280]{1,0:T(8,128)(2,1)S(1)} collective-permute-done((bf16[128,1280]{1,0:T(8,128)(2,1)S(1)}, bf16[128,1280]{1,0:T(8,128)(2,1)S(1)}, u32[]{:S(2)}, u32[]{:S(2)}) %collective-permute-start.10) | collective-permute-done | bytes 327712 | tf_op jit(solution)/shard_map/ppermute | solution.py:277
  42.8 2.7 %collective-permute-start.8 = (bf16[128,1280]{1,0:T(8,128)(2,1)S(1)}, bf16[128,1280]{1,0:T(8,128)(2,1)S(1)}, u32[]{:S(2)}, u32[]{:S(2)}) collective-permute-start(bf16[128,1280]{1,0:T(8,128)(2,1)S(1)} %collective-permute-done.6.refs_7_), channel_id=1, source_target_pairs={{0,112},{4,116},{8,120},{12,124},{16,0},{20,4},{24,8},{28,12},{32,... | collective-permute-start | bytes 983048 | tf_op jit(solution)/shard_map/ppermute | solution.py:277
  45.5 4.3 %collective-permute-done.15.refs_15_ = bf16[128,1280]{1,0:T(8,128)(2,1)S(1)} collective-permute-done((bf16[128,1280]{1,0:T(8,128)(2,1)S(1)}, bf16[128,1280]{1,0:T(8,128)(2,1)S(1)}, u32[]{:S(2)}, u32[]{:S(2)}) %collective-permute-start.15) | collective-permute-done | bytes 327712 | tf_op jit(solution)/shard_map/ppermute | solution.py:277
  49.8 2.7 %collective-permute-start.7 = (bf16[128,1280]{1,0:T(8,128)(2,1)S(1)}, bf16[128,1280]{1,0:T(8,128)(2,1)S(1)}, u32[]{:S(2)}, u32[]{:S(2)}) collective-permute-start(bf16[128,1280]{1,0:T(8,128)(2,1)S(1)} %collective-permute-done.5.refs_6_), channel_id=1, source_target_pairs={{0,112},{4,116},{8,120},{12,124},{16,0},{20,4},{24,8},{28,12},{32,... | collective-permute-start | bytes 983048 | tf_op jit(solution)/shard_map/ppermute | solution.py:277
  52.5 4.3 %collective-permute-done.11.refs_12_ = bf16[128,1280]{1,0:T(8,128)(2,1)S(1)} collective-permute-done((bf16[128,1280]{1,0:T(8,128)(2,1)S(1)}, bf16[128,1280]{1,0:T(8,128)(2,1)S(1)}, u32[]{:S(2)}, u32[]{:S(2)}) %collective-permute-start.11) | collective-permute-done | bytes 327712 | tf_op jit(solution)/shard_map/ppermute | solution.py:277
  59.5 4.3 %collective-permute-done.16.refs_13_ = bf16[128,1280]{1,0:T(8,128)(2,1)S(1)} collective-permute-done((bf16[128,1280]{1,0:T(8,128)(2,1)S(1)}, bf16[128,1280]{1,0:T(8,128)(2,1)S(1)}, u32[]{:S(2)}, u32[]{:S(2)}) %collective-permute-start.16) | collective-permute-done | bytes 327712 | tf_op jit(solution)/shard_map/ppermute | solution.py:277
  65.5 5.4 %collective-permute-done.12.refs_10_ = bf16[128,1280]{1,0:T(8,128)(2,1)S(1)} collective-permute-done((bf16[128,1280]{1,0:T(8,128)(2,1)S(1)}, bf16[128,1280]{1,0:T(8,128)(2,1)S(1)}, u32[]{:S(2)}, u32[]{:S(2)}) %collective-permute-start.12) | collective-permute-done | bytes 327712 | tf_op jit(solution)/shard_map/ppermute | solution.py:277
  70.9 4.3 %shard_map.67 = (bf16[144,1280]{1,0:T(8,128)(2,1)S(1)}, bf16[144,1280]{1,0:T(8,128)(2,1)S(1)}, bf16[144,1280]{1,0:T(8,128)(2,1)S(1)}, bf16[144,1280]{1,0:T(8,128)(2,1)S(1)}, bf16[2048,1280]{1,0:T(8,128)(2,1)S(1)}) custom-call(s32[8]{0:T(128)S(1)} %concatenate.3.sc, bf16[4,16,1280]{2,1,0:T(8,128)(2,1)S(1)} %convert_element_type.11.refs_0_, ...), custom_call_target="tpu_custom_call" | custom-call | flops 41943040 | bytes 131072 | tf_op jit(solution)/shard_map/pallas_call | solution.py:184
  79.3 4.0 %shard_map.68 = (bf16[2,128,1280]{2,1,0:T(8,128)(2,1)S(1)}, bf16[2,128,1280]{2,1,0:T(8,128)(2,1)S(1)}) custom-call(s32[8]{0:T(128)S(1)} %concatenate.3.sc, bf16[4,128,2688]{2,1,0:T(8,128)(2,1)S(1)} %collective-permute-done.22.refs_0_, bf16[2048,1280]{1,0:T(8,128)(2,1)S(1)} %get-tuple-element.63.refs_1_), custom_call_target="tpu_custom_call" | custom-call | flops 41943040 | bytes 131072 | tf_op jit(solution)/shard_map/pallas_call | solution.py:195
  85.6 4.0 %shard_map.69 = (bf16[2,128,1280]{2,1,0:T(8,128)(2,1)S(1)}, bf16[2,128,1280]{2,1,0:T(8,128)(2,1)S(1)}) custom-call(s32[8]{0:T(128)S(1)} %concatenate.3.sc, bf16[4,128,2688]{2,1,0:T(8,128)(2,1)S(1)} %collective-permute-done.20.refs_0_, bf16[2048,1280]{1,0:T(8,128)(2,1)S(1)} %get-tuple-element.63.refs_1_), custom_call_target="tpu_custom_call" | custom-call | flops 41943040 | bytes 131072 | tf_op jit(solution)/shard_map/pallas_call | solution.py:195
  91.6 4.0 %shard_map.70 = (bf16[2,128,1280]{2,1,0:T(8,128)(2,1)S(1)}, bf16[2,128,1280]{2,1,0:T(8,128)(2,1)S(1)}) custom-call(s32[8]{0:T(128)S(1)} %concatenate.3.sc, bf16[4,128,2688]{2,1,0:T(8,128)(2,1)S(1)} %collective-permute-done.21.refs_0_, bf16[2048,1280]{1,0:T(8,128)(2,1)S(1)} %get-tuple-element.63.refs_1_), custom_call_target="tpu_custom_call" | custom-call | flops 41943040 | bytes 131072 | tf_op jit(solution)/shard_map/pallas_call | solution.py:195
  95.7 14.7 %collective-permute-done.18.refs_2_ = bf16[144,1280]{1,0:T(8,128)(2,1)S(1)} collective-permute-done((bf16[144,1280]{1,0:T(8,128)(2,1)S(1)}, bf16[144,1280]{1,0:T(8,128)(2,1)S(1)}, u32[]{:S(2)}, u32[]{:S(2)}) %collective-permute-start.18) | collective-permute-done | bytes 368672 | tf_op jit(solution)/shard_map/ppermute | solution.py:273
  110.9 2.9 %collective-permute-start.23 = (bf16[144,1280]{1,0:T(8,128)(2,1)S(1)}, bf16[144,1280]{1,0:T(8,128)(2,1)S(1)}, u32[]{:S(2)}, u32[]{:S(2)}) collective-permute-start(bf16[144,1280]{1,0:T(8,128)(2,1)S(1)} %shard_map.71), channel_id=1, source_target_pairs={{0,128},{4,132},{8,136},{12,140},{16,144},{20,148},{24,152},{28,15... | collective-permute-start | bytes 1105928 | tf_op jit(solution)/shard_map/ppermute | solution.py:269
  115.5 7.5 %collective-permute-done.25.refs_1_ = bf16[128,1280]{1,0:T(8,128)(2,1)S(1)} collective-permute-done((bf16[128,1280]{1,0:T(8,128)(2,1)S(1)}, bf16[128,1280]{1,0:T(8,128)(2,1)S(1)}, u32[]{:S(2)}, u32[]{:S(2)}) %collective-permute-start.25) | collective-permute-done | bytes 327712 | tf_op jit(solution)/shard_map/ppermute | solution.py:273
  123.3 3.3 %collective-permute-start.27 = (bf16[128,1280]{1,0:T(8,128)(2,1)S(1)}, bf16[128,1280]{1,0:T(8,128)(2,1)S(1)}, u32[]{:S(2)}, u32[]{:S(2)}) collective-permute-start(bf16[128,1280]{1,0:T(8,128)(2,1)S(1)} %shard_map.74), channel_id=1, source_target_pairs={{0,132},{4,128},{8,140},{12,136},{16,148},{20,144},{24,156},{28,15... | collective-permute-start | bytes 983048 | tf_op jit(solution)/shard_map/ppermute | solution.py:269
  127.8 3.7 %collective-permute-done.28.refs_1_ = bf16[128,1280]{1,0:T(8,128)(2,1)S(1)} collective-permute-done((bf16[128,1280]{1,0:T(8,128)(2,1)S(1)}, bf16[128,1280]{1,0:T(8,128)(2,1)S(1)}, u32[]{:S(2)}, u32[]{:S(2)}) %collective-permute-start.28) | collective-permute-done | bytes 327712 | tf_op jit(solution)/shard_map/ppermute | solution.py:273
  134.4 3.0 %collective-permute-done.31.refs_1_ = bf16[128,1280]{1,0:T(8,128)(2,1)S(1)} collective-permute-done((bf16[128,1280]{1,0:T(8,128)(2,1)S(1)}, bf16[128,1280]{1,0:T(8,128)(2,1)S(1)}, u32[]{:S(2)}, u32[]{:S(2)}) %collective-permute-start.31) | collective-permute-done | bytes 327712 | tf_op jit(solution)/shard_map/ppermute | solution.py:273
  141.5 8.1 %collective-permute-done.32.refs_3_ = bf16[128,1280]{1,0:T(8,128)(2,1)S(1)} collective-permute-done((bf16[128,1280]{1,0:T(8,128)(2,1)S(1)}, bf16[128,1280]{1,0:T(8,128)(2,1)S(1)}, u32[]{:S(2)}, u32[]{:S(2)}) %collective-permute-start.32) | collective-permute-done | bytes 327712 | tf_op jit(solution)/shard_map/ppermute | solution.py:269
  (74 shorter events, 42.6 us)
Async XLA Ops:
  16.0 61.2 %collective-permute-start.20 = (bf16[4,128,2688]{2,1,0:T(8,128)(2,1)S(1)}, bf16[4,128,2688]{2,1,0:T(8,128)(2,1)S(1)}, u32[]{:S(2)}, u32[]{:S(2)}) collective-permute-start(bf16[4,128,2688]{2,1,0:T(8,128)(2,1)S(1)} %get-tuple-element.61), channel_id=1, source_target_pairs={{0,8},{4,12},{8,0},{12,4},{16,24},{20,28},{24,16},{28,20},{32,40},... | collective-permute-start | bytes 8257544 | tf_op jit(solution)/shard_map/ppermute | solution.py:264
  16.1 12.7 %collective-permute-start.9 = (bf16[128,1280]{1,0:T(8,128)(2,1)S(1)}, bf16[128,1280]{1,0:T(8,128)(2,1)S(1)}, u32[]{:S(2)}, u32[]{:S(2)}) collective-permute-start(bf16[128,1280]{1,0:T(8,128)(2,1)S(1)} %get-tuple-element.54.refs_2_), channel_id=1, source_target_pairs={{0,16},{4,20},{8,24},{12,28},{16,32},{20,36},{24,40},{28,44},{32,4... | collective-permute-start | bytes 983048 | tf_op jit(solution)/shard_map/ppermute | solution.py:277
  21.1 14.7 %collective-permute-start.14 = (bf16[128,1280]{1,0:T(8,128)(2,1)S(1)}, bf16[128,1280]{1,0:T(8,128)(2,1)S(1)}, u32[]{:S(2)}, u32[]{:S(2)}) collective-permute-start(bf16[128,1280]{1,0:T(8,128)(2,1)S(1)} %get-tuple-element.55.refs_3_), channel_id=1, source_target_pairs={{0,16},{4,20},{8,24},{12,28},{16,32},{20,36},{24,40},{28,44},{32,4... | collective-permute-start | bytes 983048 | tf_op jit(solution)/shard_map/ppermute | solution.py:277
  21.1 14.7 %collective-permute-start.3 = (bf16[128,1280]{1,0:T(8,128)(2,1)S(1)}, bf16[128,1280]{1,0:T(8,128)(2,1)S(1)}, u32[]{:S(2)}, u32[]{:S(2)}) collective-permute-start(bf16[128,1280]{1,0:T(8,128)(2,1)S(1)} %get-tuple-element.54.refs_2_), channel_id=1, source_target_pairs={{0,112},{4,116},{8,120},{12,124},{16,0},{20,4},{24,8},{28,12},{32,... | collective-permute-start | bytes 983048 | tf_op jit(solution)/shard_map/ppermute | solution.py:277
  28.7 14.0 %collective-permute-start.10 = (bf16[128,1280]{1,0:T(8,128)(2,1)S(1)}, bf16[128,1280]{1,0:T(8,128)(2,1)S(1)}, u32[]{:S(2)}, u32[]{:S(2)}) collective-permute-start(bf16[128,1280]{1,0:T(8,128)(2,1)S(1)} %collective-permute-done.9.refs_16_), channel_id=1, source_target_pairs={{0,16},{4,20},{8,24},{12,28},{16,32},{20,36},{24,40},{28,44},{32,4... | collective-permute-start | bytes 983048 | tf_op jit(solution)/shard_map/ppermute | solution.py:277
  28.7 14.0 %collective-permute-start.6 = (bf16[128,1280]{1,0:T(8,128)(2,1)S(1)}, bf16[128,1280]{1,0:T(8,128)(2,1)S(1)}, u32[]{:S(2)}, u32[]{:S(2)}) collective-permute-start(bf16[128,1280]{1,0:T(8,128)(2,1)S(1)} %collective-permute-done.4.refs_5_), channel_id=1, source_target_pairs={{0,112},{4,116},{8,120},{12,124},{16,0},{20,4},{24,8},{28,12},{32,... | collective-permute-start | bytes 983048 | tf_op jit(solution)/shard_map/ppermute | solution.py:277
  35.8 14.0 %collective-permute-start.15 = (bf16[128,1280]{1,0:T(8,128)(2,1)S(1)}, bf16[128,1280]{1,0:T(8,128)(2,1)S(1)}, u32[]{:S(2)}, u32[]{:S(2)}) collective-permute-start(bf16[128,1280]{1,0:T(8,128)(2,1)S(1)} %collective-permute-done.14.refs_17_), channel_id=1, source_target_pairs={{0,16},{4,20},{8,24},{12,28},{16,32},{20,36},{24,40},{28,44},{32,4... | collective-permute-start | bytes 983048 | tf_op jit(solution)/shard_map/ppermute | solution.py:277
  35.8 14.0 %collective-permute-start.5 = (bf16[128,1280]{1,0:T(8,128)(2,1)S(1)}, bf16[128,1280]{1,0:T(8,128)(2,1)S(1)}, u32[]{:S(2)}, u32[]{:S(2)}) collective-permute-start(bf16[128,1280]{1,0:T(8,128)(2,1)S(1)} %collective-permute-done.3.refs_4_), channel_id=1, source_target_pairs={{0,112},{4,116},{8,120},{12,124},{16,0},{20,4},{24,8},{28,12},{32,... | collective-permute-start | bytes 983048 | tf_op jit(solution)/shard_map/ppermute | solution.py:277
  42.8 14.0 %collective-permute-start.11 = (bf16[128,1280]{1,0:T(8,128)(2,1)S(1)}, bf16[128,1280]{1,0:T(8,128)(2,1)S(1)}, u32[]{:S(2)}, u32[]{:S(2)}) collective-permute-start(bf16[128,1280]{1,0:T(8,128)(2,1)S(1)} %collective-permute-done.10.refs_14_), channel_id=1, source_target_pairs={{0,16},{4,20},{8,24},{12,28},{16,32},{20,36},{24,40},{28,44},{32,4... | collective-permute-start | bytes 983048 | tf_op jit(solution)/shard_map/ppermute | solution.py:277
  42.8 14.0 %collective-permute-start.8 = (bf16[128,1280]{1,0:T(8,128)(2,1)S(1)}, bf16[128,1280]{1,0:T(8,128)(2,1)S(1)}, u32[]{:S(2)}, u32[]{:S(2)}) collective-permute-start(bf16[128,1280]{1,0:T(8,128)(2,1)S(1)} %collective-permute-done.6.refs_7_), channel_id=1, source_target_pairs={{0,112},{4,116},{8,120},{12,124},{16,0},{20,4},{24,8},{28,12},{32,... | collective-permute-start | bytes 983048 | tf_op jit(solution)/shard_map/ppermute | solution.py:277
  49.8 14.0 %collective-permute-start.16 = (bf16[128,1280]{1,0:T(8,128)(2,1)S(1)}, bf16[128,1280]{1,0:T(8,128)(2,1)S(1)}, u32[]{:S(2)}, u32[]{:S(2)}) collective-permute-start(bf16[128,1280]{1,0:T(8,128)(2,1)S(1)} %collective-permute-done.15.refs_15_), channel_id=1, source_target_pairs={{0,16},{4,20},{8,24},{12,28},{16,32},{20,36},{24,40},{28,44},{32,4... | collective-permute-start | bytes 983048 | tf_op jit(solution)/shard_map/ppermute | solution.py:277
  49.8 15.7 %collective-permute-start.7 = (bf16[128,1280]{1,0:T(8,128)(2,1)S(1)}, bf16[128,1280]{1,0:T(8,128)(2,1)S(1)}, u32[]{:S(2)}, u32[]{:S(2)}) collective-permute-start(bf16[128,1280]{1,0:T(8,128)(2,1)S(1)} %collective-permute-done.5.refs_6_), channel_id=1, source_target_pairs={{0,112},{4,116},{8,120},{12,124},{16,0},{20,4},{24,8},{28,12},{32,... | collective-permute-start | bytes 983048 | tf_op jit(solution)/shard_map/ppermute | solution.py:277
  56.8 14.0 %collective-permute-start.12 = (bf16[128,1280]{1,0:T(8,128)(2,1)S(1)}, bf16[128,1280]{1,0:T(8,128)(2,1)S(1)}, u32[]{:S(2)}, u32[]{:S(2)}) collective-permute-start(bf16[128,1280]{1,0:T(8,128)(2,1)S(1)} %collective-permute-done.11.refs_12_), channel_id=1, source_target_pairs={{0,16},{4,20},{8,24},{12,28},{16,32},{20,36},{24,40},{28,44},{32,4... | collective-permute-start | bytes 983048 | tf_op jit(solution)/shard_map/ppermute | solution.py:277
  56.8 14.0 %collective-permute-start.13 = (bf16[128,1280]{1,0:T(8,128)(2,1)S(1)}, bf16[128,1280]{1,0:T(8,128)(2,1)S(1)}, u32[]{:S(2)}, u32[]{:S(2)}) collective-permute-start(bf16[128,1280]{1,0:T(8,128)(2,1)S(1)} %collective-permute-done.8.refs_9_), channel_id=1, source_target_pairs={{0,112},{4,116},{8,120},{12,124},{16,0},{20,4},{24,8},{28,12},{32,... | collective-permute-start | bytes 983048 | tf_op jit(solution)/shard_map/ppermute | solution.py:277
  63.8 15.5 %collective-permute-start.22 = (bf16[4,128,2688]{2,1,0:T(8,128)(2,1)S(1)}, bf16[4,128,2688]{2,1,0:T(8,128)(2,1)S(1)}, u32[]{:S(2)}, u32[]{:S(2)}) collective-permute-start(bf16[4,128,2688]{2,1,0:T(8,128)(2,1)S(1)} %get-tuple-element.46.refs_1_), channel_id=1, source_target_pairs={{0,4},{4,0},{8,12},{12,8},{16,20},{20,16},{24,28},{28,24},{32,36},... | collective-permute-start | bytes 8257544 | tf_op jit(solution)/shard_map/ppermute | solution.py:264
  77.1 12.5 %collective-permute-start.21 = (bf16[4,128,2688]{2,1,0:T(8,128)(2,1)S(1)}, bf16[4,128,2688]{2,1,0:T(8,128)(2,1)S(1)}, u32[]{:S(2)}, u32[]{:S(2)}) collective-permute-start(bf16[4,128,2688]{2,1,0:T(8,128)(2,1)S(1)} %collective-permute-done.20.refs_0_), channel_id=1, source_target_pairs={{0,4},{4,0},{8,12},{12,8},{16,20},{20,16},{24,28},{28,24},{32,36},... | collective-permute-start | bytes 8257544 | tf_op jit(solution)/shard_map/ppermute | solution.py:264
  78.1 17.5 %collective-permute-start.17 = (bf16[144,1280]{1,0:T(8,128)(2,1)S(1)}, bf16[144,1280]{1,0:T(8,128)(2,1)S(1)}, u32[]{:S(2)}, u32[]{:S(2)}) collective-permute-start(bf16[144,1280]{1,0:T(8,128)(2,1)S(1)} %get-tuple-element.57), channel_id=1, source_target_pairs={{0,2},{1,3},{2,0},{3,1},{4,6},{5,7},{6,4},{7,5},{8,10},{9,11},{10,... | collective-permute-start | bytes 1105928 | tf_op jit(solution)/shard_map/ppermute | solution.py:273
  83.3 30.4 %collective-permute-start.24 = (bf16[2,128,1280]{2,1,0:T(8,128)(2,1)S(1)}, bf16[2,128,1280]{2,1,0:T(8,128)(2,1)S(1)}, u32[]{:S(2)}, u32[]{:S(2)}) collective-permute-start(bf16[2,128,1280]{2,1,0:T(8,128)(2,1)S(1)} %get-tuple-element.72), channel_id=1, source_target_pairs={{0,1},{1,0},{2,3},{3,2},{4,5},{5,4},{6,7},{7,6},{8,9},{9,8},{10,11... | collective-permute-start | bytes 1966088 | tf_op jit(solution)/shard_map/ppermute | solution.py:273
  83.8 26.6 %collective-permute-start.18 = (bf16[144,1280]{1,0:T(8,128)(2,1)S(1)}, bf16[144,1280]{1,0:T(8,128)(2,1)S(1)}, u32[]{:S(2)}, u32[]{:S(2)}) collective-permute-start(bf16[144,1280]{1,0:T(8,128)(2,1)S(1)} %get-tuple-element.58), channel_id=1, source_target_pairs={{0,1},{1,0},{2,3},{3,2},{4,5},{5,4},{6,7},{7,6},{8,9},{9,8},{10,11... | collective-permute-start | bytes 1105928 | tf_op jit(solution)/shard_map/ppermute | solution.py:273
  84.9 25.5 %collective-permute-start.19 = (bf16[144,1280]{1,0:T(8,128)(2,1)S(1)}, bf16[144,1280]{1,0:T(8,128)(2,1)S(1)}, u32[]{:S(2)}, u32[]{:S(2)}) collective-permute-start(bf16[144,1280]{1,0:T(8,128)(2,1)S(1)} %get-tuple-element.59), channel_id=1, source_target_pairs={{0,3},{1,2},{2,1},{3,0},{4,7},{5,6},{6,5},{7,4},{8,11},{9,10},{10,... | collective-permute-start | bytes 1105928 | tf_op jit(solution)/shard_map/ppermute | solution.py:273
  89.6 24.4 %collective-permute-start.26 = (bf16[2,128,1280]{2,1,0:T(8,128)(2,1)S(1)}, bf16[2,128,1280]{2,1,0:T(8,128)(2,1)S(1)}, u32[]{:S(2)}, u32[]{:S(2)}) collective-permute-start(bf16[2,128,1280]{2,1,0:T(8,128)(2,1)S(1)} %get-tuple-element.76), channel_id=1, source_target_pairs={{0,3},{1,2},{2,1},{3,0},{4,7},{5,6},{6,5},{7,4},{8,11},{9,10},{10,... | collective-permute-start | bytes 1966088 | tf_op jit(solution)/shard_map/ppermute | solution.py:273
  95.6 31.0 %collective-permute-start.30 = (bf16[2,128,1280]{2,1,0:T(8,128)(2,1)S(1)}, bf16[2,128,1280]{2,1,0:T(8,128)(2,1)S(1)}, u32[]{:S(2)}, u32[]{:S(2)}) collective-permute-start(bf16[2,128,1280]{2,1,0:T(8,128)(2,1)S(1)} %get-tuple-element.82), channel_id=1, source_target_pairs={{0,1},{1,0},{2,3},{3,2},{4,5},{5,4},{6,7},{7,6},{8,9},{9,8},{10,11... | collective-permute-start | bytes 1966088 | tf_op jit(solution)/shard_map/ppermute | solution.py:273
  110.9 12.1 %collective-permute-start.23 = (bf16[144,1280]{1,0:T(8,128)(2,1)S(1)}, bf16[144,1280]{1,0:T(8,128)(2,1)S(1)}, u32[]{:S(2)}, u32[]{:S(2)}) collective-permute-start(bf16[144,1280]{1,0:T(8,128)(2,1)S(1)} %shard_map.71), channel_id=1, source_target_pairs={{0,128},{4,132},{8,136},{12,140},{16,144},{20,148},{24,152},{28,15... | collective-permute-start | bytes 1105928 | tf_op jit(solution)/shard_map/ppermute | solution.py:269
  114.2 17.3 %collective-permute-start.28 = (bf16[128,1280]{1,0:T(8,128)(2,1)S(1)}, bf16[128,1280]{1,0:T(8,128)(2,1)S(1)}, u32[]{:S(2)}, u32[]{:S(2)}) collective-permute-start(bf16[128,1280]{1,0:T(8,128)(2,1)S(1)} %get-tuple-element.78), channel_id=1, source_target_pairs={{0,1},{1,0},{2,3},{3,2},{4,5},{5,4},{6,7},{7,6},{8,9},{9,8},{10,11... | collective-permute-start | bytes 983048 | tf_op jit(solution)/shard_map/ppermute | solution.py:273
  (13 other events, 114.9 us)
where the time goes:
time: 152 us
  waiting for transfers between devices  73.8 us (49%)
  starting transfers between devices  48.2 us (32%)
  Pallas kernels  23.3 us (15%)
  local copies, waits for them, and re-layouts  5.04 us (3%)
  other arithmetic  1.59 us (1%)
    ppermute x14, waiting for transfers between devices, along_z(): lax.ppermute(value, 'dp', [(i, (i + steps * GROUP) % DP) for i in range(D...  32.1 us
    ppermute x9, waiting for transfers between devices, along_y(): return lax.ppermute(value, 'tensor', [(i, i ^ offset) for i in range(N_T)])  28.8 us
    ppermute x14, starting transfers between devices, along_z(): lax.ppermute(value, 'dp', [(i, (i + steps * GROUP) % DP) for i in range(D...  21.1 us
    pallas_call x3, Pallas kernels, product(): local(functools.partial(product_body, kind, False), [bf16(2, TILE, BOTH)]...  11.9 us
    ppermute x4, starting transfers between devices, cross(): return lax.ppermute(value, ('section', 'dp'), pairs)  11.2 us
    ppermute x4, waiting for transfers between devices, cross(): return lax.ppermute(value, ('section', 'dp'), pairs)  9.28 us
    ppermute x9, starting transfers between devices, along_y(): return lax.ppermute(value, 'tensor', [(i, i ^ offset) for i in range(N_T)])  8.05 us
    ppermute x6, starting transfers between devices, swap(): return lax.ppermute(value, 'dp', [(i, i ^ offset) for i in range(DP)])  7.81 us
  transfers between devices with their start and end apart: 33, of which 15 were waited for; matrix products, arithmetic and copies ran while one was open for 1% of the time, Pallas kernels for 13%

commit v1 on v0

--- a/solution.py
+++ b/solution.py
@@ -18,6 +18,7 @@
 DEPTH = 2048
 FULL = 5120
 ROOT = 1.0 / math.sqrt(TILE)
+CONFIG = {'kinds': (2, 0, 1, 0), 'order': ('P0', 'P1', 'P2', 'T0', 'P3', 'M1', 'M2', 'T1', 'M3', 'T2', 'T3'), 'crossed': ((0, 'T1'), (1, 'T3')), 'far': 'P0', 'hold': {}, 'sends': (2, 1, 3)}
 MORE = 16
 BOTH = 2 * WIDE
 VMEM_LIMIT = 20 * 1024 * 1024
@@ -79,33 +80,41 @@
         copy.wait()
 
 
-def moving(body, out_shape, n_in, n_copies, cost):
+def moving(body, out_shape, n_in, n_copies, cost, smem=1, vmem=VMEM_LIMIT):
     return pl.pallas_call(
         body,
         out_shape=out_shape,
-        in_specs=[pl.BlockSpec(memory_space=pltpu.SMEM)] + [pl.BlockSpec(memory_space=pl.ANY)] * n_in,
+        in_specs=[pl.BlockSpec(memory_space=pltpu.SMEM)] * smem + [pl.BlockSpec(memory_space=pl.ANY)] * n_in,
         out_specs=jax.tree.map(lambda _: pl.BlockSpec(memory_space=pltpu.VMEM), out_shape),
         scratch_shapes=[pltpu.SemaphoreType.DMA((n_copies,))],
-        compiler_params=pltpu.CompilerParams(vmem_limit_bytes=VMEM_LIMIT),
+        compiler_params=pltpu.CompilerParams(vmem_limit_bytes=vmem),
         cost_estimate=cost,
     )
 
 
-def split_weight_body(sc, w_ref, *refs):
+def split_weight_body(w_ref, *refs):
+    own = lax.axis_index("dp") % GROUP
     copies = []
     for p, out in enumerate(refs[:GROUP]):
+        to = own ^ p
         for u in range(2):
-            start = ((2 * (sc[2] ^ (p & 1)) + u) * 2 + (sc[1] ^ (p >> 1))) * WIDE
+            start = ((2 * (to % 2) + u) * 2 + to // 2) * WIDE
             part = w_ref.at[:, pl.ds(pl.multiple_of(start, TILE), WIDE)]
             copies.append((part, out.at[:, pl.ds(u * WIDE, WIDE)]))
     copy_all(copies, refs[GROUP])
 
 
-def split_weight(sc, weight):
+def split_weight(weight):
     rows = weight.shape[0]
-    return moving(split_weight_body, [bf16(rows, BOTH)] * GROUP, 1, 2 * GROUP, cost_of(0, 4 * rows * FULL))(
-        sc, weight
-    )
+    return moving(
+        split_weight_body,
+        [bf16(rows, BOTH)] * GROUP,
+        1,
+        2 * GROUP,
+        cost_of(0, 4 * rows * FULL),
+        smem=0,
+        vmem=VMEM_LIMIT,
+    )(weight)
 
 
 def join_weight_body(sc, *refs):
@@ -180,24 +189,24 @@
 PRODUCT_COST = cost_of(2 * N_T * TILE * DEPTH * BOTH, 8 * MIB)
 
 
+def parts_of(kind, rows):
+    return [bf16(rows, BOTH)] * N_T if kind == PLAIN else [bf16(2, rows, BOTH)] * 2
+
+
 def first_product(sc, kind, top, left, blocks):
     outs = local(
         functools.partial(product_body, kind, True),
-        [bf16(TILE + MORE, BOTH)] * N_T + [bf16(DEPTH, BOTH)],
+        [*parts_of(kind, TILE + MORE), bf16(DEPTH, BOTH)],
         2 + len(blocks),
         smem=1,
         cost=PRODUCT_COST,
     )(sc, top, left, *blocks)
-    return outs[:N_T], outs[N_T]
+    return outs[:-1], outs[-1]
 
 
 def product(sc, kind, left, weight):
     return local(
-        functools.partial(product_body, kind, False),
-        [bf16(2, TILE, BOTH)] * 2,
-        2,
-        smem=1,
-        cost=PRODUCT_COST,
+        functools.partial(product_body, kind, False), parts_of(kind, TILE), 2, smem=1, cost=PRODUCT_COST
     )(sc, left, weight)
 
 
@@ -231,33 +240,45 @@
     )(table, *parts)
 
 
-def finish_body(sc, h_ref, *refs):
-    pieces, out, lim = refs[:GROUP], refs[GROUP], refs[GROUP + 1]
-    lim[...] = pieces[0][TILE:, :].astype(jnp.float32)
-    for p, piece in enumerate(pieces):
+def finish_body(which, sc, h_ref, *refs):
+    n = len(which)
+    pieces, first_ref, out, done, sems = refs[:n], refs[n], refs[-3], refs[-2], refs[-1]
+    lim = first_ref[TILE:, :].astype(jnp.float32)
+    copies = []
+    for i, (p, piece) in enumerate(zip(which, pieces)):
         half = sc[1] ^ (p >> 1)
         for u in range(2):
             tensor = 2 * (sc[2] ^ (p & 1)) + u
-            k = sc[0] ^ tensor
-            top = lim[pl.ds(k, 1), pl.ds(pl.multiple_of(half * WIDE, TILE), WIDE)]
-            first = tensor * 10 + half * (WIDE // TILE)
+            row = jax.lax.broadcasted_iota(jnp.int32, (MORE, WIDE), 0) == sc[0] ^ tensor
+            tops = jnp.where(half == 0, lim[:, :WIDE], lim[:, WIDE:])
+            top = jnp.sum(jnp.where(row, tops, 0.0), axis=0, keepdims=True)
+            slot = 2 * i + u
             for j in range(WIDE // TILE):
                 limit = top[:, j * TILE : (j + 1) * TILE]
                 value = piece[:TILE, u * WIDE + j * TILE : u * WIDE + (j + 1) * TILE].astype(jnp.float32)
                 value = jnp.clip(value, -limit, limit).astype(jnp.bfloat16)
                 value = jnp.dot(value, h_ref[...], preferred_element_type=jnp.float32)
-                out[:, pl.ds(pl.multiple_of((first + j) * TILE, TILE), TILE)] = value * ROOT
-
-
-def finish(sc, table, pieces):
-    return local(
-        finish_body,
-        jax.ShapeDtypeStruct((TILE, FULL), jnp.float32),
-        1 + GROUP,
-        smem=1,
-        scratch=[pltpu.VMEM((MORE, BOTH), jnp.float32)],
-        cost=cost_of(2 * TILE * TILE * FULL, 4 * MIB),
-    )(sc, table, *pieces)
+                done[slot, :, j * TILE : (j + 1) * TILE] = value * ROOT
+            start = pl.multiple_of((tensor * 2 + half) * WIDE, TILE)
+            copies.append(pltpu.make_async_copy(done.at[slot], out.at[:, pl.ds(start, WIDE)], sems.at[slot]))
+            copies[-1].start()
+    for copy in copies:
+        copy.wait()
+
+
+def finish(sc, table, which, pieces, first, out=None):
+    vmem, n = pl.BlockSpec(memory_space=pltpu.VMEM), len(which)
+    older = [] if out is None else [out]
+    return pl.pallas_call(
+        functools.partial(finish_body, which),
+        out_shape=jax.ShapeDtypeStruct((TILE, FULL), jnp.float32),
+        in_specs=[pl.BlockSpec(memory_space=pltpu.SMEM)] + [vmem] * (2 + n) + [pl.BlockSpec(memory_space=pl.ANY)] * len(older),
+        out_specs=pl.BlockSpec(memory_space=pl.ANY),
+        scratch_shapes=[pltpu.VMEM((2 * n, TILE, WIDE), jnp.float32), pltpu.SemaphoreType.DMA((2 * n,))],
+        input_output_aliases={3 + n: 0} if older else {},
+        compiler_params=pltpu.CompilerParams(vmem_limit_bytes=VMEM_LIMIT),
+        cost_estimate=cost_of(2 * TILE * TILE * FULL, 4 * MIB),
+    )(sc, table, *pieces, first, *older)
 
 
 def swap(value, offset):
@@ -306,54 +327,71 @@
             perm[0, 0],
         ]
     )
-    pieces = split_weight(sc, weight[0])
+    pieces = split_weight(weight[0])
     swapped = [None] + [swap(pieces[p], p) for p in range(1, GROUP)]
     top = limits(expo[0], perm[0, 0])
 
     near, far = order_left(sc, left[0], base[0])
-    near_c = swap(near, 1)
-
-    held = [{0: b} for b in join_weight(sc, [pieces[0], *chain(swapped[1:], near, top)])]
+
+    held = [{0: b} for b in join_weight(sc, [pieces[0], *chain(swapped[1:], near, far, top)])]
     far_x = swap(after(far, held[1][0]), 2)
     for s in range(1, 4):
         for h in held:
             h[N_Z - s], h[s] = along_z(h[(N_Z - s + 1) % N_Z], 1), along_z(h[s - 1], -1)
+    near_c = swap(after(near, held[0][3], held[0][5]), 1)
     held[0][4] = along_z(held[0][5], 1)
     held[1][4] = along_z(held[1][3], -1)
 
-    def begin(parts, kind):
-        return parts[0], along_y(parts[1], STEPS[kind][0]), kind
-
-    def middle(begun, *wait):
-        keep, got, kind = begun
-        (got,) = chain((got,), *wait)
-        stay, leave = add(keep, got)
-        return stay, along_y(leave, STEPS[kind][1]), leave
-
-    def end(middled, *wait):
-        stay, got, _ = middled
-        (got,) = chain((got,), *wait)
-        return turn(table, stay, got)
-
-    own, w = first_product(sc, PLAIN, top, near, [held[side][j] for j in range(N_Z) for side in range(2)])
-    own_got = [along_y(own[k], k) for k in (2, 1, 3)]
-    other = begin(product(sc, 0, near_c, w), 0)
-    far_x = after(far_x, own[0])
-    far_xc = swap(far_x, 1)
-    across = begin(product(sc, 1, after(far_x, other[0]), w), 1)
-    last = begin(product(sc, 0, after(far_xc, across[0]), w), 0)
-    own_t = turn(table, own[0], *chain(own_got, last[0]))
-    own_x = cross(own_t, 0)
-    other = middle(other, own_t)
-    across = middle(across, other[2])
-    other_t = end(other, across[2], own_x)
-    other_x = cross(other_t, 1)
-    across_t = end(across, other_t)
-    across_x = cross(across_t, 2)
-    last = middle(last, across[2])
-    last_t = end(last, across_t, other_x)
-    last_x = cross(last_t, 3)
-    return finish(sc, table, (own_x, other_x, across_x, last_x))[None]
+    kinds, order = CONFIG["kinds"], CONFIG["order"]
+    parts, sent, far, turned, crossed, outputs = {}, {}, {}, {}, {}, {}
+    lefts = {0: near, 1: near_c}
+    last = []
+
+    def take(values, name):
+        wait = last + [crossed[i] for i, by in CONFIG["crossed"] if by == name]
+        return chain(values, *wait) if wait else values
+
+    def send(i, *wait):
+        if kinds[i] == PLAIN:
+            sent[i] = {k: along_y(*chain((parts[i][k],), *wait), k) for k in CONFIG["sends"]}
+        else:
+            sent[i] = along_y(*chain((parts[i][1],), *wait), STEPS[kinds[i]][0])
+
+    for name in order:
+        step, i = name[0], int(name[1])
+        kind = kinds[i]
+        if step == "P":
+            if i == 0:
+                parts[i], w = first_product(sc, kind, top, near, [held[side][j] for j in range(N_Z) for side in range(2)])
+            else:
+                (left,) = take((lefts[i],), name)
+                parts[i] = product(sc, kind, left, w)
+            if i not in CONFIG["hold"]:
+                send(i)
+            mark = parts[i][0]
+            if name == CONFIG["far"]:
+                lefts[2] = after(far_x, mark)
+                lefts[3] = swap(lefts[2], 1)
+        elif step == "M":
+            (got,) = take((sent[i],), name)
+            stay, leave = add(parts[i][0], got)
+            far[i] = (stay, along_y(leave, STEPS[kind][1]))
+            mark = leave
+        else:
+            if kind == PLAIN:
+                turned[i] = turn(table, parts[i][0], *take([sent[i][k] for k in (1, 2, 3)], name))
+            else:
+                (got,) = take((far[i][1],), name)
+                turned[i] = turn(table, far[i][0], got)
+            crossed[i] = cross(turned[i], i)
+            mark = turned[i]
+        last = [mark]
+        for j, by in CONFIG["hold"].items():
+            if by == name:
+                send(j, mark)
+    first, second = chain((crossed[0], crossed[1]), *last), (crossed[2], crossed[3])
+    result = finish(sc, table, (0, 1), first, first[0])
+    return finish(sc, table, (2, 3), chain(second, result), first[0], result)[None]
 
 
 def solution(mesh):

time: 152 us -> 151 us (level)
  waiting for transfers between devices: 73.8 us -> 68.3 us
  starting transfers between devices: 48.2 us -> 51.1 us
    ppermute x14, waiting for transfers between devices: 32.1 us -> 29.4 us  [along_z(): lax.ppermute(value, 'dp', [(i, (i + steps * GROUP) % DP) for i in range(D...]
    ppermute x9, waiting for transfers between devices: 28.8 us -> 26.2 us  [along_y(): return lax.ppermute(value, 'tensor', [(i, i ^ offset) for i in range(N_T)])]
    pallas_call x5 -> x6, Pallas kernels: 18.9 us -> 20 us  [the longest x3 12 us: product(): local(functools.partial(product_body, kind, False), parts_of(kind, TILE),...]
  transfers between devices with their start and end apart: 33 -> 33, of which waited for: 15 -> 19; matrix products, arithmetic and copies ran while one was open for 1% -> 2% of each run, Pallas kernels for 13% -> 14%
where the time goes in v1:
time: 151 us; the launch traced here: 150 us
  waiting for transfers between devices  68.3 us (45%)
  starting transfers between devices  51.1 us (34%)
  Pallas kernels  23.9 us (16%)
  local copies, waits for them, and re-layouts  5.05 us (3%)
  other arithmetic  1.6 us (1%)
    ppermute x14, waiting for transfers between devices, along_z(): lax.ppermute(value, 'dp', [(i, (i + steps * GROUP) % DP) for i in range(D...  29.4 us
    ppermute x9, waiting for transfers between devices, along_y(): return lax.ppermute(value, 'tensor', [(i, i ^ offset) for i in range(N_T)])  26.2 us
    ppermute x14, starting transfers between devices, along_z(): lax.ppermute(value, 'dp', [(i, (i + steps * GROUP) % DP) for i in range(D...  22.1 us
    pallas_call x3, Pallas kernels, product(): local(functools.partial(product_body, kind, False), parts_of(kind, TILE),...  12 us
    ppermute x4, starting transfers between devices, cross(): return lax.ppermute(value, ('section', 'dp'), pairs)  11.5 us
    ppermute x9, starting transfers between devices, along_y(): return lax.ppermute(value, 'tensor', [(i, i ^ offset) for i in range(N_T)])  9.06 us
    ppermute x4, waiting for transfers between devices, cross(): return lax.ppermute(value, ('section', 'dp'), pairs)  8.83 us
    ppermute x6, starting transfers between devices, swap(): return lax.ppermute(value, 'dp', [(i, i ^ offset) for i in range(DP)])  8.45 us
  transfers between devices with their start and end apart: 33, of which 19 were waited for; matrix products, arithmetic and copies ran while one was open for 2% of the time, Pallas kernels for 14%

profile of v1, /device:TPU:1, one launch (start us, length us, event | category | flops | bytes accessed | tf_op | source)
XLA Modules:
  0.0 150.3 jit_solution(4646279282655048693)
XLA Ops:
  1.3 3.3 %collective-permute-start = (bf16[64,1280]{1,0:T(8,128)(2,1)S(1)}, bf16[64,1280]{1,0:T(8,128)(2,1)S(1)}, u32[]{:S(2)}, u32[]{:S(2)}) collective-permute-start(bf16[64,1280]{1,0:T(8,128)(2,1)S(1)} %get-tuple-element.54), channel_id=1, source_target_pairs={{0,4},{4,0},{8,12},{12,8},{16,20},{20,16},{24,28},{28,24},{32,36},... | collective-permute-start | bytes 491528 | tf_op jit(solution)/shard_map/ppermute | solution.py:285
  15.9 3.9 %collective-permute-start.5 = (bf16[128,1280]{1,0:T(8,128)(2,1)S(1)}, bf16[128,1280]{1,0:T(8,128)(2,1)S(1)}, u32[]{:S(2)}, u32[]{:S(2)}) collective-permute-start(bf16[128,1280]{1,0:T(8,128)(2,1)S(1)} %get-tuple-element.61.refs_3_), channel_id=1, source_target_pairs={{0,112},{4,116},{8,120},{12,124},{16,0},{20,4},{24,8},{28,12},{32,... | collective-permute-start | bytes 983048 | tf_op jit(solution)/shard_map/ppermute | solution.py:298
  21.3 6.2 %collective-permute-done.10.refs_16_ = bf16[128,1280]{1,0:T(8,128)(2,1)S(1)} collective-permute-done((bf16[128,1280]{1,0:T(8,128)(2,1)S(1)}, bf16[128,1280]{1,0:T(8,128)(2,1)S(1)}, u32[]{:S(2)}, u32[]{:S(2)}) %collective-permute-start.10) | collective-permute-done | bytes 327712 | tf_op jit(solution)/shard_map/ppermute | solution.py:298
  30.1 3.3 %collective-permute-done.4.refs_4_ = bf16[128,1280]{1,0:T(8,128)(2,1)S(1)} collective-permute-done((bf16[128,1280]{1,0:T(8,128)(2,1)S(1)}, bf16[128,1280]{1,0:T(8,128)(2,1)S(1)}, u32[]{:S(2)}, u32[]{:S(2)}) %collective-permute-start.4) | collective-permute-done | bytes 327712 | tf_op jit(solution)/shard_map/ppermute | solution.py:298
  33.4 3.4 %collective-permute-start.6 = (bf16[128,1280]{1,0:T(8,128)(2,1)S(1)}, bf16[128,1280]{1,0:T(8,128)(2,1)S(1)}, u32[]{:S(2)}, u32[]{:S(2)}) collective-permute-start(bf16[128,1280]{1,0:T(8,128)(2,1)S(1)} %collective-permute-done.4.refs_4_), channel_id=1, source_target_pairs={{0,112},{4,116},{8,120},{12,124},{16,0},{20,4},{24,8},{28,12},{32,... | collective-permute-start | bytes 983048 | tf_op jit(solution)/shard_map/ppermute | solution.py:298
  36.8 4.7 %collective-permute-done.11.refs_14_ = bf16[128,1280]{1,0:T(8,128)(2,1)S(1)} collective-permute-done((bf16[128,1280]{1,0:T(8,128)(2,1)S(1)}, bf16[128,1280]{1,0:T(8,128)(2,1)S(1)}, u32[]{:S(2)}, u32[]{:S(2)}) %collective-permute-start.11) | collective-permute-done | bytes 327712 | tf_op jit(solution)/shard_map/ppermute | solution.py:298
  44.2 3.3 %collective-permute-done.6.refs_6_ = bf16[128,1280]{1,0:T(8,128)(2,1)S(1)} collective-permute-done((bf16[128,1280]{1,0:T(8,128)(2,1)S(1)}, bf16[128,1280]{1,0:T(8,128)(2,1)S(1)}, u32[]{:S(2)}, u32[]{:S(2)}) %collective-permute-start.6) | collective-permute-done | bytes 327712 | tf_op jit(solution)/shard_map/ppermute | solution.py:298
  47.5 3.4 %collective-permute-start.8 = (bf16[128,1280]{1,0:T(8,128)(2,1)S(1)}, bf16[128,1280]{1,0:T(8,128)(2,1)S(1)}, u32[]{:S(2)}, u32[]{:S(2)}) collective-permute-start(bf16[128,1280]{1,0:T(8,128)(2,1)S(1)} %collective-permute-done.6.refs_6_), channel_id=1, source_target_pairs={{0,112},{4,116},{8,120},{12,124},{16,0},{20,4},{24,8},{28,12},{32,... | collective-permute-start | bytes 983048 | tf_op jit(solution)/shard_map/ppermute | solution.py:298
  50.9 3.6 %collective-permute-done.12.refs_12_ = bf16[128,1280]{1,0:T(8,128)(2,1)S(1)} collective-permute-done((bf16[128,1280]{1,0:T(8,128)(2,1)S(1)}, bf16[128,1280]{1,0:T(8,128)(2,1)S(1)}, u32[]{:S(2)}, u32[]{:S(2)}) %collective-permute-start.12) | collective-permute-done | bytes 327712 | tf_op jit(solution)/shard_map/ppermute | solution.py:298
  54.5 3.4 %collective-permute-start.14 = (bf16[128,1280]{1,0:T(8,128)(2,1)S(1)}, bf16[128,1280]{1,0:T(8,128)(2,1)S(1)}, u32[]{:S(2)}, u32[]{:S(2)}) collective-permute-start(bf16[128,1280]{1,0:T(8,128)(2,1)S(1)} %collective-permute-done.9.refs_9_), channel_id=1, source_target_pairs={{0,112},{4,116},{8,120},{12,124},{16,0},{20,4},{24,8},{28,12},{32,... | collective-permute-start | bytes 983048 | tf_op jit(solution)/shard_map/ppermute | solution.py:298
  57.9 3.6 %collective-permute-done.8.refs_8_ = bf16[128,1280]{1,0:T(8,128)(2,1)S(1)} collective-permute-done((bf16[128,1280]{1,0:T(8,128)(2,1)S(1)}, bf16[128,1280]{1,0:T(8,128)(2,1)S(1)}, u32[]{:S(2)}, u32[]{:S(2)}) %collective-permute-start.8) | collective-permute-done | bytes 327712 | tf_op jit(solution)/shard_map/ppermute | solution.py:298
  63.8 4.7 %collective-permute-done.13.refs_10_ = bf16[128,1280]{1,0:T(8,128)(2,1)S(1)} collective-permute-done((bf16[128,1280]{1,0:T(8,128)(2,1)S(1)}, bf16[128,1280]{1,0:T(8,128)(2,1)S(1)}, u32[]{:S(2)}, u32[]{:S(2)}) %collective-permute-start.13) | collective-permute-done | bytes 327712 | tf_op jit(solution)/shard_map/ppermute | solution.py:298
  68.5 4.3 %shard_map.67 = (bf16[144,1280]{1,0:T(8,128)(2,1)S(1)}, bf16[144,1280]{1,0:T(8,128)(2,1)S(1)}, bf16[144,1280]{1,0:T(8,128)(2,1)S(1)}, bf16[144,1280]{1,0:T(8,128)(2,1)S(1)}, bf16[2048,1280]{1,0:T(8,128)(2,1)S(1)}) custom-call(s32[8]{0:T(128)S(1)} %concatenate.3.sc, bf16[4,16,1280]{2,1,0:T(8,128)(2,1)S(1)} %convert_element_type.11.refs_0_, ...), custom_call_target="tpu_custom_call" | custom-call | flops 41943040 | bytes 131072 | tf_op jit(solution)/shard_map/pallas_call | solution.py:197
  72.9 3.0 %collective-permute-done.3.refs_0_ = bf16[4,128,2688]{2,1,0:T(8,128)(2,1)S(1)} collective-permute-done((bf16[4,128,2688]{2,1,0:T(8,128)(2,1)S(1)}, bf16[4,128,2688]{2,1,0:T(8,128)(2,1)S(1)}, u32[]{:S(2)}, u32[]{:S(2)}) %collective-permute-start.3) | collective-permute-done | bytes 2752544 | tf_op jit(solution)/shard_map/ppermute | solution.py:285
  80.1 4.0 %shard_map.68 = (bf16[2,128,1280]{2,1,0:T(8,128)(2,1)S(1)}, bf16[2,128,1280]{2,1,0:T(8,128)(2,1)S(1)}) custom-call(s32[8]{0:T(128)S(1)} %concatenate.3.sc, bf16[4,128,2688]{2,1,0:T(8,128)(2,1)S(1)} %collective-permute-done.18.refs_0_, bf16[2048,1280]{1,0:T(8,128)(2,1)S(1)} %get-tuple-element.68.refs_1_), custom_call_target="tpu_custom_call" | custom-call | flops 41943040 | bytes 131072 | tf_op jit(solution)/shard_map/pallas_call | solution.py:208
  84.4 4.0 %shard_map.69 = (bf16[2,128,1280]{2,1,0:T(8,128)(2,1)S(1)}, bf16[2,128,1280]{2,1,0:T(8,128)(2,1)S(1)}) custom-call(s32[8]{0:T(128)S(1)} %concatenate.3.sc, bf16[4,128,2688]{2,1,0:T(8,128)(2,1)S(1)} %collective-permute-done.3.refs_0_, bf16[2048,1280]{1,0:T(8,128)(2,1)S(1)} %get-tuple-element.68.refs_1_), custom_call_target="tpu_custom_call" | custom-call | flops 41943040 | bytes 131072 | tf_op jit(solution)/shard_map/pallas_call | solution.py:208
  88.6 6.5 %collective-permute-done.22.refs_1_ = bf16[144,1280]{1,0:T(8,128)(2,1)S(1)} collective-permute-done((bf16[144,1280]{1,0:T(8,128)(2,1)S(1)}, bf16[144,1280]{1,0:T(8,128)(2,1)S(1)}, u32[]{:S(2)}, u32[]{:S(2)}) %collective-permute-start.22) | collective-permute-done | bytes 368672 | tf_op jit(solution)/shard_map/ppermute | solution.py:294
  98.3 4.0 %shard_map.71 = (bf16[2,128,1280]{2,1,0:T(8,128)(2,1)S(1)}, bf16[2,128,1280]{2,1,0:T(8,128)(2,1)S(1)}) custom-call(s32[8]{0:T(128)S(1)} %concatenate.3.sc, bf16[4,128,2688]{2,1,0:T(8,128)(2,1)S(1)} %collective-permute-done.21.refs_0_, bf16[2048,1280]{1,0:T(8,128)(2,1)S(1)} %get-tuple-element.68.refs_1_), custom_call_target="tpu_custom_call" | custom-call | flops 41943040 | bytes 131072 | tf_op jit(solution)/shard_map/pallas_call | solution.py:208
  102.4 2.9 %collective-permute-start.28 = (bf16[144,1280]{1,0:T(8,128)(2,1)S(1)}, bf16[144,1280]{1,0:T(8,128)(2,1)S(1)}, u32[]{:S(2)}, u32[]{:S(2)}) collective-permute-start(bf16[144,1280]{1,0:T(8,128)(2,1)S(1)} %shard_map.70), channel_id=1, source_target_pairs={{0,128},{4,132},{8,136},{12,140},{16,144},{20,148},{24,152},{28,15... | collective-permute-start | bytes 1105928 | tf_op jit(solution)/shard_map/ppermute | solution.py:290
  105.2 3.9 %collective-permute-done.20.b_ref = bf16[2,128,1280]{2,1,0:T(8,128)(2,1)S(1)} collective-permute-done((bf16[2,128,1280]{2,1,0:T(8,128)(2,1)S(1)}, bf16[2,128,1280]{2,1,0:T(8,128)(2,1)S(1)}, u32[]{:S(2)}, u32[]{:S(2)}) %collective-permute-start.20) | collective-permute-done | bytes 655392 | tf_op jit(solution)/shard_map/ppermute | solution.py:294
  114.1 6.7 %collective-permute-done.27.refs_1_ = bf16[128,1280]{1,0:T(8,128)(2,1)S(1)} collective-permute-done((bf16[128,1280]{1,0:T(8,128)(2,1)S(1)}, bf16[128,1280]{1,0:T(8,128)(2,1)S(1)}, u32[]{:S(2)}, u32[]{:S(2)}) %collective-permute-start.27) | collective-permute-done | bytes 327712 | tf_op jit(solution)/shard_map/ppermute | solution.py:294
  126.5 3.7 %collective-permute-done.25.refs_1_ = bf16[128,1280]{1,0:T(8,128)(2,1)S(1)} collective-permute-done((bf16[128,1280]{1,0:T(8,128)(2,1)S(1)}, bf16[128,1280]{1,0:T(8,128)(2,1)S(1)}, u32[]{:S(2)}, u32[]{:S(2)}) %collective-permute-start.25) | collective-permute-done | bytes 327712 | tf_op jit(solution)/shard_map/ppermute | solution.py:294
  134.2 3.3 %collective-permute-start.32 = (bf16[128,1280]{1,0:T(8,128)(2,1)S(1)}, bf16[128,1280]{1,0:T(8,128)(2,1)S(1)}, u32[]{:S(2)}, u32[]{:S(2)}) collective-permute-start(bf16[128,1280]{1,0:T(8,128)(2,1)S(1)} %shard_map.77), channel_id=1, source_target_pairs={{0,140},{4,136},{8,132},{12,128},{16,156},{20,152},{24,148},{28,14... | collective-permute-start | bytes 983048 | tf_op jit(solution)/shard_map/ppermute | solution.py:290
  140.2 8.1 %collective-permute-done.32.refs_1_ = bf16[128,1280]{1,0:T(8,128)(2,1)S(1)} collective-permute-done((bf16[128,1280]{1,0:T(8,128)(2,1)S(1)}, bf16[128,1280]{1,0:T(8,128)(2,1)S(1)}, u32[]{:S(2)}, u32[]{:S(2)}) %collective-permute-start.32) | collective-permute-done | bytes 327712 | tf_op jit(solution)/shard_map/ppermute | solution.py:290
  (75 shorter events, 48.8 us)
Async XLA Ops:
  14.7 61.2 %collective-permute-start.3 = (bf16[4,128,2688]{2,1,0:T(8,128)(2,1)S(1)}, bf16[4,128,2688]{2,1,0:T(8,128)(2,1)S(1)}, u32[]{:S(2)}, u32[]{:S(2)}) collective-permute-start(bf16[4,128,2688]{2,1,0:T(8,128)(2,1)S(1)} %get-tuple-element.62), channel_id=1, source_target_pairs={{0,8},{4,12},{8,0},{12,4},{16,24},{20,28},{24,16},{28,20},{32,40},... | collective-permute-start | bytes 8257544 | tf_op jit(solution)/shard_map/ppermute | solution.py:285
  14.8 12.7 %collective-permute-start.10 = (bf16[128,1280]{1,0:T(8,128)(2,1)S(1)}, bf16[128,1280]{1,0:T(8,128)(2,1)S(1)}, u32[]{:S(2)}, u32[]{:S(2)}) collective-permute-start(bf16[128,1280]{1,0:T(8,128)(2,1)S(1)} %get-tuple-element.63.refs_2_), channel_id=1, source_target_pairs={{0,16},{4,20},{8,24},{12,28},{16,32},{20,36},{24,40},{28,44},{32,4... | collective-permute-start | bytes 983048 | tf_op jit(solution)/shard_map/ppermute | solution.py:298
  19.8 13.6 %collective-permute-start.4 = (bf16[128,1280]{1,0:T(8,128)(2,1)S(1)}, bf16[128,1280]{1,0:T(8,128)(2,1)S(1)}, u32[]{:S(2)}, u32[]{:S(2)}) collective-permute-start(bf16[128,1280]{1,0:T(8,128)(2,1)S(1)} %get-tuple-element.63.refs_2_), channel_id=1, source_target_pairs={{0,112},{4,116},{8,120},{12,124},{16,0},{20,4},{24,8},{28,12},{32,... | collective-permute-start | bytes 983048 | tf_op jit(solution)/shard_map/ppermute | solution.py:298
  21.3 15.6 %collective-permute-start.15 = (bf16[128,1280]{1,0:T(8,128)(2,1)S(1)}, bf16[128,1280]{1,0:T(8,128)(2,1)S(1)}, u32[]{:S(2)}, u32[]{:S(2)}) collective-permute-start(bf16[128,1280]{1,0:T(8,128)(2,1)S(1)} %get-tuple-element.61.refs_3_), channel_id=1, source_target_pairs={{0,16},{4,20},{8,24},{12,28},{16,32},{20,36},{24,40},{28,44},{32,4... | collective-permute-start | bytes 983048 | tf_op jit(solution)/shard_map/ppermute | solution.py:298
  27.4 14.0 %collective-permute-start.11 = (bf16[128,1280]{1,0:T(8,128)(2,1)S(1)}, bf16[128,1280]{1,0:T(8,128)(2,1)S(1)}, u32[]{:S(2)}, u32[]{:S(2)}) collective-permute-start(bf16[128,1280]{1,0:T(8,128)(2,1)S(1)} %collective-permute-done.10.refs_16_), channel_id=1, source_target_pairs={{0,16},{4,20},{8,24},{12,28},{16,32},{20,36},{24,40},{28,44},{32,4... | collective-permute-start | bytes 983048 | tf_op jit(solution)/shard_map/ppermute | solution.py:298
  27.5 14.0 %collective-permute-start.7 = (bf16[128,1280]{1,0:T(8,128)(2,1)S(1)}, bf16[128,1280]{1,0:T(8,128)(2,1)S(1)}, u32[]{:S(2)}, u32[]{:S(2)}) collective-permute-start(bf16[128,1280]{1,0:T(8,128)(2,1)S(1)} %collective-permute-done.5.refs_5_), channel_id=1, source_target_pairs={{0,112},{4,116},{8,120},{12,124},{16,0},{20,4},{24,8},{28,12},{32,... | collective-permute-start | bytes 983048 | tf_op jit(solution)/shard_map/ppermute | solution.py:298
  33.4 14.0 %collective-permute-start.6 = (bf16[128,1280]{1,0:T(8,128)(2,1)S(1)}, bf16[128,1280]{1,0:T(8,128)(2,1)S(1)}, u32[]{:S(2)}, u32[]{:S(2)}) collective-permute-start(bf16[128,1280]{1,0:T(8,128)(2,1)S(1)} %collective-permute-done.4.refs_4_), channel_id=1, source_target_pairs={{0,112},{4,116},{8,120},{12,124},{16,0},{20,4},{24,8},{28,12},{32,... | collective-permute-start | bytes 983048 | tf_op jit(solution)/shard_map/ppermute | solution.py:298
  36.8 14.0 %collective-permute-start.16 = (bf16[128,1280]{1,0:T(8,128)(2,1)S(1)}, bf16[128,1280]{1,0:T(8,128)(2,1)S(1)}, u32[]{:S(2)}, u32[]{:S(2)}) collective-permute-start(bf16[128,1280]{1,0:T(8,128)(2,1)S(1)} %collective-permute-done.15.refs_17_), channel_id=1, source_target_pairs={{0,16},{4,20},{8,24},{12,28},{16,32},{20,36},{24,40},{28,44},{32,4... | collective-permute-start | bytes 983048 | tf_op jit(solution)/shard_map/ppermute | solution.py:298
  41.5 12.9 %collective-permute-start.12 = (bf16[128,1280]{1,0:T(8,128)(2,1)S(1)}, bf16[128,1280]{1,0:T(8,128)(2,1)S(1)}, u32[]{:S(2)}, u32[]{:S(2)}) collective-permute-start(bf16[128,1280]{1,0:T(8,128)(2,1)S(1)} %collective-permute-done.11.refs_14_), channel_id=1, source_target_pairs={{0,16},{4,20},{8,24},{12,28},{16,32},{20,36},{24,40},{28,44},{32,4... | collective-permute-start | bytes 983048 | tf_op jit(solution)/shard_map/ppermute | solution.py:298
  41.5 13.0 %collective-permute-start.9 = (bf16[128,1280]{1,0:T(8,128)(2,1)S(1)}, bf16[128,1280]{1,0:T(8,128)(2,1)S(1)}, u32[]{:S(2)}, u32[]{:S(2)}) collective-permute-start(bf16[128,1280]{1,0:T(8,128)(2,1)S(1)} %collective-permute-done.7.refs_7_), channel_id=1, source_target_pairs={{0,112},{4,116},{8,120},{12,124},{16,0},{20,4},{24,8},{28,12},{32,... | collective-permute-start | bytes 983048 | tf_op jit(solution)/shard_map/ppermute | solution.py:298
  47.5 14.0 %collective-permute-start.8 = (bf16[128,1280]{1,0:T(8,128)(2,1)S(1)}, bf16[128,1280]{1,0:T(8,128)(2,1)S(1)}, u32[]{:S(2)}, u32[]{:S(2)}) collective-permute-start(bf16[128,1280]{1,0:T(8,128)(2,1)S(1)} %collective-permute-done.6.refs_6_), channel_id=1, source_target_pairs={{0,112},{4,116},{8,120},{12,124},{16,0},{20,4},{24,8},{28,12},{32,... | collective-permute-start | bytes 983048 | tf_op jit(solution)/shard_map/ppermute | solution.py:298
  50.9 12.9 %collective-permute-start.17 = (bf16[128,1280]{1,0:T(8,128)(2,1)S(1)}, bf16[128,1280]{1,0:T(8,128)(2,1)S(1)}, u32[]{:S(2)}, u32[]{:S(2)}) collective-permute-start(bf16[128,1280]{1,0:T(8,128)(2,1)S(1)} %collective-permute-done.16.refs_15_), channel_id=1, source_target_pairs={{0,16},{4,20},{8,24},{12,28},{16,32},{20,36},{24,40},{28,44},{32,4... | collective-permute-start | bytes 983048 | tf_op jit(solution)/shard_map/ppermute | solution.py:298
  54.4 14.0 %collective-permute-start.13 = (bf16[128,1280]{1,0:T(8,128)(2,1)S(1)}, bf16[128,1280]{1,0:T(8,128)(2,1)S(1)}, u32[]{:S(2)}, u32[]{:S(2)}) collective-permute-start(bf16[128,1280]{1,0:T(8,128)(2,1)S(1)} %collective-permute-done.12.refs_12_), channel_id=1, source_target_pairs={{0,16},{4,20},{8,24},{12,28},{16,32},{20,36},{24,40},{28,44},{32,4... | collective-permute-start | bytes 983048 | tf_op jit(solution)/shard_map/ppermute | solution.py:298
  54.5 14.0 %collective-permute-start.14 = (bf16[128,1280]{1,0:T(8,128)(2,1)S(1)}, bf16[128,1280]{1,0:T(8,128)(2,1)S(1)}, u32[]{:S(2)}, u32[]{:S(2)}) collective-permute-start(bf16[128,1280]{1,0:T(8,128)(2,1)S(1)} %collective-permute-done.9.refs_9_), channel_id=1, source_target_pairs={{0,112},{4,116},{8,120},{12,124},{16,0},{20,4},{24,8},{28,12},{32,... | collective-permute-start | bytes 983048 | tf_op jit(solution)/shard_map/ppermute | solution.py:298
  61.5 18.6 %collective-permute-start.18 = (bf16[4,128,2688]{2,1,0:T(8,128)(2,1)S(1)}, bf16[4,128,2688]{2,1,0:T(8,128)(2,1)S(1)}, u32[]{:S(2)}, u32[]{:S(2)}) collective-permute-start(bf16[4,128,2688]{2,1,0:T(8,128)(2,1)S(1)} %get-tuple-element.66.refs_1_), channel_id=1, source_target_pairs={{0,4},{4,0},{8,12},{12,8},{16,20},{20,16},{24,28},{28,24},{32,36},... | collective-permute-start | bytes 8257544 | tf_op jit(solution)/shard_map/ppermute | solution.py:285
  75.8 22.4 %collective-permute-start.21 = (bf16[4,128,2688]{2,1,0:T(8,128)(2,1)S(1)}, bf16[4,128,2688]{2,1,0:T(8,128)(2,1)S(1)}, u32[]{:S(2)}, u32[]{:S(2)}) collective-permute-start(bf16[4,128,2688]{2,1,0:T(8,128)(2,1)S(1)} %collective-permute-done.3.refs_0_), channel_id=1, source_target_pairs={{0,4},{4,0},{8,12},{12,8},{16,20},{20,16},{24,28},{28,24},{32,36},... | collective-permute-start | bytes 8257544 | tf_op jit(solution)/shard_map/ppermute | solution.py:285
  78.0 17.1 %collective-permute-start.22 = (bf16[144,1280]{1,0:T(8,128)(2,1)S(1)}, bf16[144,1280]{1,0:T(8,128)(2,1)S(1)}, u32[]{:S(2)}, u32[]{:S(2)}) collective-permute-start(bf16[144,1280]{1,0:T(8,128)(2,1)S(1)} %get-tuple-element.74), channel_id=1, source_target_pairs={{0,1},{1,0},{2,3},{3,2},{4,5},{5,4},{6,7},{7,6},{8,9},{9,8},{10,11... | collective-permute-start | bytes 1105928 | tf_op jit(solution)/shard_map/ppermute | solution.py:294
  78.4 18.3 %collective-permute-start.24 = (bf16[144,1280]{1,0:T(8,128)(2,1)S(1)}, bf16[144,1280]{1,0:T(8,128)(2,1)S(1)}, u32[]{:S(2)}, u32[]{:S(2)}) collective-permute-start(bf16[144,1280]{1,0:T(8,128)(2,1)S(1)} %get-tuple-element.76), channel_id=1, source_target_pairs={{0,3},{1,2},{2,1},{3,0},{4,7},{5,6},{6,5},{7,4},{8,11},{9,10},{10,... | collective-permute-start | bytes 1105928 | tf_op jit(solution)/shard_map/ppermute | solution.py:294
  84.1 25.0 %collective-permute-start.20 = (bf16[2,128,1280]{2,1,0:T(8,128)(2,1)S(1)}, bf16[2,128,1280]{2,1,0:T(8,128)(2,1)S(1)}, u32[]{:S(2)}, u32[]{:S(2)}) collective-permute-start(bf16[2,128,1280]{2,1,0:T(8,128)(2,1)S(1)} %get-tuple-element.73), channel_id=1, source_target_pairs={{0,1},{1,0},{2,3},{3,2},{4,5},{5,4},{6,7},{7,6},{8,9},{9,8},{10,11... | collective-permute-start | bytes 1966088 | tf_op jit(solution)/shard_map/ppermute | solution.py:294
  96.8 17.0 %collective-permute-start.19 = (bf16[2,128,1280]{2,1,0:T(8,128)(2,1)S(1)}, bf16[2,128,1280]{2,1,0:T(8,128)(2,1)S(1)}, u32[]{:S(2)}, u32[]{:S(2)}) collective-permute-start(bf16[2,128,1280]{2,1,0:T(8,128)(2,1)S(1)} %get-tuple-element.72), channel_id=1, source_target_pairs={{0,3},{1,2},{2,1},{3,0},{4,7},{5,6},{6,5},{7,4},{8,11},{9,10},{10,... | collective-permute-start | bytes 1966088 | tf_op jit(solution)/shard_map/ppermute | solution.py:294
  102.3 21.5 %collective-permute-start.26 = (bf16[2,128,1280]{2,1,0:T(8,128)(2,1)S(1)}, bf16[2,128,1280]{2,1,0:T(8,128)(2,1)S(1)}, u32[]{:S(2)}, u32[]{:S(2)}) collective-permute-start(bf16[2,128,1280]{2,1,0:T(8,128)(2,1)S(1)} %get-tuple-element.87), channel_id=1, source_target_pairs={{0,1},{1,0},{2,3},{3,2},{4,5},{5,4},{6,7},{7,6},{8,9},{9,8},{10,11... | collective-permute-start | bytes 1966088 | tf_op jit(solution)/shard_map/ppermute | solution.py:294
  114.0 16.2 %collective-permute-start.25 = (bf16[128,1280]{1,0:T(8,128)(2,1)S(1)}, bf16[128,1280]{1,0:T(8,128)(2,1)S(1)}, u32[]{:S(2)}, u32[]{:S(2)}) collective-permute-start(bf16[128,1280]{1,0:T(8,128)(2,1)S(1)} %get-tuple-element.86), channel_id=1, source_target_pairs={{0,1},{1,0},{2,3},{3,2},{4,5},{5,4},{6,7},{7,6},{8,9},{9,8},{10,11... | collective-permute-start | bytes 983048 | tf_op jit(solution)/shard_map/ppermute | solution.py:294
  121.1 12.0 %collective-permute-start.31 = (bf16[128,1280]{1,0:T(8,128)(2,1)S(1)}, bf16[128,1280]{1,0:T(8,128)(2,1)S(1)}, u32[]{:S(2)}, u32[]{:S(2)}) collective-permute-start(bf16[128,1280]{1,0:T(8,128)(2,1)S(1)} %shard_map.74), channel_id=1, source_target_pairs={{0,132},{4,128},{8,140},{12,136},{16,148},{20,144},{24,156},{28,15... | collective-permute-start | bytes 983048 | tf_op jit(solution)/shard_map/ppermute | solution.py:290
  134.2 14.0 %collective-permute-start.32 = (bf16[128,1280]{1,0:T(8,128)(2,1)S(1)}, bf16[128,1280]{1,0:T(8,128)(2,1)S(1)}, u32[]{:S(2)}, u32[]{:S(2)}) collective-permute-start(bf16[128,1280]{1,0:T(8,128)(2,1)S(1)} %shard_map.77), channel_id=1, source_target_pairs={{0,140},{4,136},{8,132},{12,128},{16,156},{20,152},{24,148},{28,14... | collective-permute-start | bytes 983048 | tf_op jit(solution)/shard_map/ppermute | solution.py:290
  (13 other events, 113.3 us)

commit v2 on v1

--- a/solution.py
+++ b/solution.py
@@ -391,7 +391,8 @@
                 send(j, mark)
     first, second = chain((crossed[0], crossed[1]), *last), (crossed[2], crossed[3])
     result = finish(sc, table, (0, 1), first, first[0])
-    return finish(sc, table, (2, 3), chain(second, result), first[0], result)[None]
+    result = finish(sc, table, (2,), chain(second[:1], result), first[0], result)
+    return finish(sc, table, (3,), chain(second[1:], result), first[0], result)[None]
 
 
 def solution(mesh):

time: 151 us -> 150 us (level)
  waiting for transfers between devices: 68.3 us -> 66.7 us
    ppermute x4, waiting for transfers between devices: 8.83 us -> 7.23 us  [cross(): return lax.ppermute(value, ('section', 'dp'), pairs)]
    pallas_call x2 -> x3, Pallas kernels: 3.71 us -> 5.05 us  [finish(): pl.pallas_call(functools.partial(finish_body, which), out_shape=jax.Shape...]
  transfers between devices with their start and end apart: 33 -> 33, of which waited for: 19 -> 19; matrix products, arithmetic and copies ran while one was open for 2% -> 2% of each run, Pallas kernels for 14% -> 15%
where the time goes in v2:
time: 150 us
  waiting for transfers between devices  66.7 us (44%)
  starting transfers between devices  51.1 us (34%)
  Pallas kernels  25.2 us (17%)
  local copies, waits for them, and re-layouts  5.05 us (3%)
  other arithmetic  1.6 us (1%)
    ppermute x14, waiting for transfers between devices, along_z(): lax.ppermute(value, 'dp', [(i, (i + steps * GROUP) % DP) for i in range(D...  29.4 us
    ppermute x9, waiting for transfers between devices, along_y(): return lax.ppermute(value, 'tensor', [(i, i ^ offset) for i in range(N_T)])  26.2 us
    ppermute x14, starting transfers between devices, along_z(): lax.ppermute(value, 'dp', [(i, (i + steps * GROUP) % DP) for i in range(D...  22.1 us
    pallas_call x3, Pallas kernels, product(): local(functools.partial(product_body, kind, False), parts_of(kind, TILE),...  12 us
    ppermute x4, starting transfers between devices, cross(): return lax.ppermute(value, ('section', 'dp'), pairs)  11.5 us
    ppermute x9, starting transfers between devices, along_y(): return lax.ppermute(value, 'tensor', [(i, i ^ offset) for i in range(N_T)])  9.06 us
    ppermute x6, starting transfers between devices, swap(): return lax.ppermute(value, 'dp', [(i, i ^ offset) for i in range(DP)])  8.45 us
    ppermute x4, waiting for transfers between devices, cross(): return lax.ppermute(value, ('section', 'dp'), pairs)  7.23 us
  transfers between devices with their start and end apart: 33, of which 19 were waited for; matrix products, arithmetic and copies ran while one was open for 2% of the time, Pallas kernels for 15%

profile of v2, /device:TPU:1, one launch (start us, length us, event | category | flops | bytes accessed | tf_op | source)
XLA Modules:
  0.0 150.1 jit_solution(126294394284397824)
XLA Ops:
  1.3 3.3 %collective-permute-start = (bf16[64,1280]{1,0:T(8,128)(2,1)S(1)}, bf16[64,1280]{1,0:T(8,128)(2,1)S(1)}, u32[]{:S(2)}, u32[]{:S(2)}) collective-permute-start(bf16[64,1280]{1,0:T(8,128)(2,1)S(1)} %get-tuple-element.54), channel_id=1, source_target_pairs={{0,4},{4,0},{8,12},{12,8},{16,20},{20,16},{24,28},{28,24},{32,36},... | collective-permute-start | bytes 491528 | tf_op jit(solution)/shard_map/ppermute | solution.py:285
  15.9 3.9 %collective-permute-start.5 = (bf16[128,1280]{1,0:T(8,128)(2,1)S(1)}, bf16[128,1280]{1,0:T(8,128)(2,1)S(1)}, u32[]{:S(2)}, u32[]{:S(2)}) collective-permute-start(bf16[128,1280]{1,0:T(8,128)(2,1)S(1)} %get-tuple-element.61.refs_3_), channel_id=1, source_target_pairs={{0,112},{4,116},{8,120},{12,124},{16,0},{20,4},{24,8},{28,12},{32,... | collective-permute-start | bytes 983048 | tf_op jit(solution)/shard_map/ppermute | solution.py:298
  21.3 6.2 %collective-permute-done.10.refs_16_ = bf16[128,1280]{1,0:T(8,128)(2,1)S(1)} collective-permute-done((bf16[128,1280]{1,0:T(8,128)(2,1)S(1)}, bf16[128,1280]{1,0:T(8,128)(2,1)S(1)}, u32[]{:S(2)}, u32[]{:S(2)}) %collective-permute-start.10) | collective-permute-done | bytes 327712 | tf_op jit(solution)/shard_map/ppermute | solution.py:298
  30.1 3.3 %collective-permute-done.4.refs_4_ = bf16[128,1280]{1,0:T(8,128)(2,1)S(1)} collective-permute-done((bf16[128,1280]{1,0:T(8,128)(2,1)S(1)}, bf16[128,1280]{1,0:T(8,128)(2,1)S(1)}, u32[]{:S(2)}, u32[]{:S(2)}) %collective-permute-start.4) | collective-permute-done | bytes 327712 | tf_op jit(solution)/shard_map/ppermute | solution.py:298
  33.4 3.4 %collective-permute-start.6 = (bf16[128,1280]{1,0:T(8,128)(2,1)S(1)}, bf16[128,1280]{1,0:T(8,128)(2,1)S(1)}, u32[]{:S(2)}, u32[]{:S(2)}) collective-permute-start(bf16[128,1280]{1,0:T(8,128)(2,1)S(1)} %collective-permute-done.4.refs_4_), channel_id=1, source_target_pairs={{0,112},{4,116},{8,120},{12,124},{16,0},{20,4},{24,8},{28,12},{32,... | collective-permute-start | bytes 983048 | tf_op jit(solution)/shard_map/ppermute | solution.py:298
  36.8 4.7 %collective-permute-done.11.refs_14_ = bf16[128,1280]{1,0:T(8,128)(2,1)S(1)} collective-permute-done((bf16[128,1280]{1,0:T(8,128)(2,1)S(1)}, bf16[128,1280]{1,0:T(8,128)(2,1)S(1)}, u32[]{:S(2)}, u32[]{:S(2)}) %collective-permute-start.11) | collective-permute-done | bytes 327712 | tf_op jit(solution)/shard_map/ppermute | solution.py:298
  44.2 3.3 %collective-permute-done.6.refs_6_ = bf16[128,1280]{1,0:T(8,128)(2,1)S(1)} collective-permute-done((bf16[128,1280]{1,0:T(8,128)(2,1)S(1)}, bf16[128,1280]{1,0:T(8,128)(2,1)S(1)}, u32[]{:S(2)}, u32[]{:S(2)}) %collective-permute-start.6) | collective-permute-done | bytes 327712 | tf_op jit(solution)/shard_map/ppermute | solution.py:298
  47.5 3.4 %collective-permute-start.8 = (bf16[128,1280]{1,0:T(8,128)(2,1)S(1)}, bf16[128,1280]{1,0:T(8,128)(2,1)S(1)}, u32[]{:S(2)}, u32[]{:S(2)}) collective-permute-start(bf16[128,1280]{1,0:T(8,128)(2,1)S(1)} %collective-permute-done.6.refs_6_), channel_id=1, source_target_pairs={{0,112},{4,116},{8,120},{12,124},{16,0},{20,4},{24,8},{28,12},{32,... | collective-permute-start | bytes 983048 | tf_op jit(solution)/shard_map/ppermute | solution.py:298
  50.9 3.6 %collective-permute-done.12.refs_12_ = bf16[128,1280]{1,0:T(8,128)(2,1)S(1)} collective-permute-done((bf16[128,1280]{1,0:T(8,128)(2,1)S(1)}, bf16[128,1280]{1,0:T(8,128)(2,1)S(1)}, u32[]{:S(2)}, u32[]{:S(2)}) %collective-permute-start.12) | collective-permute-done | bytes 327712 | tf_op jit(solution)/shard_map/ppermute | solution.py:298
  54.5 3.4 %collective-permute-start.14 = (bf16[128,1280]{1,0:T(8,128)(2,1)S(1)}, bf16[128,1280]{1,0:T(8,128)(2,1)S(1)}, u32[]{:S(2)}, u32[]{:S(2)}) collective-permute-start(bf16[128,1280]{1,0:T(8,128)(2,1)S(1)} %collective-permute-done.9.refs_9_), channel_id=1, source_target_pairs={{0,112},{4,116},{8,120},{12,124},{16,0},{20,4},{24,8},{28,12},{32,... | collective-permute-start | bytes 983048 | tf_op jit(solution)/shard_map/ppermute | solution.py:298
  57.9 3.6 %collective-permute-done.8.refs_8_ = bf16[128,1280]{1,0:T(8,128)(2,1)S(1)} collective-permute-done((bf16[128,1280]{1,0:T(8,128)(2,1)S(1)}, bf16[128,1280]{1,0:T(8,128)(2,1)S(1)}, u32[]{:S(2)}, u32[]{:S(2)}) %collective-permute-start.8) | collective-permute-done | bytes 327712 | tf_op jit(solution)/shard_map/ppermute | solution.py:298
  63.8 4.7 %collective-permute-done.13.refs_10_ = bf16[128,1280]{1,0:T(8,128)(2,1)S(1)} collective-permute-done((bf16[128,1280]{1,0:T(8,128)(2,1)S(1)}, bf16[128,1280]{1,0:T(8,128)(2,1)S(1)}, u32[]{:S(2)}, u32[]{:S(2)}) %collective-permute-start.13) | collective-permute-done | bytes 327712 | tf_op jit(solution)/shard_map/ppermute | solution.py:298
  68.5 4.3 %shard_map.67 = (bf16[144,1280]{1,0:T(8,128)(2,1)S(1)}, bf16[144,1280]{1,0:T(8,128)(2,1)S(1)}, bf16[144,1280]{1,0:T(8,128)(2,1)S(1)}, bf16[144,1280]{1,0:T(8,128)(2,1)S(1)}, bf16[2048,1280]{1,0:T(8,128)(2,1)S(1)}) custom-call(s32[8]{0:T(128)S(1)} %concatenate.3.sc, bf16[4,16,1280]{2,1,0:T(8,128)(2,1)S(1)} %convert_element_type.11.refs_0_, ...), custom_call_target="tpu_custom_call" | custom-call | flops 41943040 | bytes 131072 | tf_op jit(solution)/shard_map/pallas_call | solution.py:197
  72.9 3.0 %collective-permute-done.3.refs_0_ = bf16[4,128,2688]{2,1,0:T(8,128)(2,1)S(1)} collective-permute-done((bf16[4,128,2688]{2,1,0:T(8,128)(2,1)S(1)}, bf16[4,128,2688]{2,1,0:T(8,128)(2,1)S(1)}, u32[]{:S(2)}, u32[]{:S(2)}) %collective-permute-start.3) | collective-permute-done | bytes 2752544 | tf_op jit(solution)/shard_map/ppermute | solution.py:285
  80.1 4.0 %shard_map.68 = (bf16[2,128,1280]{2,1,0:T(8,128)(2,1)S(1)}, bf16[2,128,1280]{2,1,0:T(8,128)(2,1)S(1)}) custom-call(s32[8]{0:T(128)S(1)} %concatenate.3.sc, bf16[4,128,2688]{2,1,0:T(8,128)(2,1)S(1)} %collective-permute-done.22.refs_0_, bf16[2048,1280]{1,0:T(8,128)(2,1)S(1)} %get-tuple-element.71.refs_1_), custom_call_target="tpu_custom_call" | custom-call | flops 41943040 | bytes 131072 | tf_op jit(solution)/shard_map/pallas_call | solution.py:208
  84.4 4.0 %shard_map.69 = (bf16[2,128,1280]{2,1,0:T(8,128)(2,1)S(1)}, bf16[2,128,1280]{2,1,0:T(8,128)(2,1)S(1)}) custom-call(s32[8]{0:T(128)S(1)} %concatenate.3.sc, bf16[4,128,2688]{2,1,0:T(8,128)(2,1)S(1)} %collective-permute-done.3.refs_0_, bf16[2048,1280]{1,0:T(8,128)(2,1)S(1)} %get-tuple-element.71.refs_1_), custom_call_target="tpu_custom_call" | custom-call | flops 41943040 | bytes 131072 | tf_op jit(solution)/shard_map/pallas_call | solution.py:208
  88.6 6.5 %collective-permute-done.19.refs_1_ = bf16[144,1280]{1,0:T(8,128)(2,1)S(1)} collective-permute-done((bf16[144,1280]{1,0:T(8,128)(2,1)S(1)}, bf16[144,1280]{1,0:T(8,128)(2,1)S(1)}, u32[]{:S(2)}, u32[]{:S(2)}) %collective-permute-start.19) | collective-permute-done | bytes 368672 | tf_op jit(solution)/shard_map/ppermute | solution.py:294
  98.3 4.0 %shard_map.71 = (bf16[2,128,1280]{2,1,0:T(8,128)(2,1)S(1)}, bf16[2,128,1280]{2,1,0:T(8,128)(2,1)S(1)}) custom-call(s32[8]{0:T(128)S(1)} %concatenate.3.sc, bf16[4,128,2688]{2,1,0:T(8,128)(2,1)S(1)} %collective-permute-done.18.refs_0_, bf16[2048,1280]{1,0:T(8,128)(2,1)S(1)} %get-tuple-element.71.refs_1_), custom_call_target="tpu_custom_call" | custom-call | flops 41943040 | bytes 131072 | tf_op jit(solution)/shard_map/pallas_call | solution.py:208
  102.4 2.9 %collective-permute-start.27 = (bf16[144,1280]{1,0:T(8,128)(2,1)S(1)}, bf16[144,1280]{1,0:T(8,128)(2,1)S(1)}, u32[]{:S(2)}, u32[]{:S(2)}) collective-permute-start(bf16[144,1280]{1,0:T(8,128)(2,1)S(1)} %shard_map.70), channel_id=1, source_target_pairs={{0,128},{4,132},{8,136},{12,140},{16,144},{20,148},{24,152},{28,15... | collective-permute-start | bytes 1105928 | tf_op jit(solution)/shard_map/ppermute | solution.py:290
  105.2 3.9 %collective-permute-done.24.b_ref = bf16[2,128,1280]{2,1,0:T(8,128)(2,1)S(1)} collective-permute-done((bf16[2,128,1280]{2,1,0:T(8,128)(2,1)S(1)}, bf16[2,128,1280]{2,1,0:T(8,128)(2,1)S(1)}, u32[]{:S(2)}, u32[]{:S(2)}) %collective-permute-start.24) | collective-permute-done | bytes 655392 | tf_op jit(solution)/shard_map/ppermute | solution.py:294
  114.1 6.7 %collective-permute-done.25.refs_1_ = bf16[128,1280]{1,0:T(8,128)(2,1)S(1)} collective-permute-done((bf16[128,1280]{1,0:T(8,128)(2,1)S(1)}, bf16[128,1280]{1,0:T(8,128)(2,1)S(1)}, u32[]{:S(2)}, u32[]{:S(2)}) %collective-permute-start.25) | collective-permute-done | bytes 327712 | tf_op jit(solution)/shard_map/ppermute | solution.py:294
  126.5 3.7 %collective-permute-done.29.refs_1_ = bf16[128,1280]{1,0:T(8,128)(2,1)S(1)} collective-permute-done((bf16[128,1280]{1,0:T(8,128)(2,1)S(1)}, bf16[128,1280]{1,0:T(8,128)(2,1)S(1)}, u32[]{:S(2)}, u32[]{:S(2)}) %collective-permute-start.29) | collective-permute-done | bytes 327712 | tf_op jit(solution)/shard_map/ppermute | solution.py:294
  134.2 3.3 %collective-permute-start.31 = (bf16[128,1280]{1,0:T(8,128)(2,1)S(1)}, bf16[128,1280]{1,0:T(8,128)(2,1)S(1)}, u32[]{:S(2)}, u32[]{:S(2)}) collective-permute-start(bf16[128,1280]{1,0:T(8,128)(2,1)S(1)} %shard_map.77), channel_id=1, source_target_pairs={{0,140},{4,136},{8,132},{12,128},{16,156},{20,152},{24,148},{28,14... | collective-permute-start | bytes 983048 | tf_op jit(solution)/shard_map/ppermute | solution.py:290
  141.8 6.5 %collective-permute-done.31.refs_0_ = bf16[128,1280]{1,0:T(8,128)(2,1)S(1)} collective-permute-done((bf16[128,1280]{1,0:T(8,128)(2,1)S(1)}, bf16[128,1280]{1,0:T(8,128)(2,1)S(1)}, u32[]{:S(2)}, u32[]{:S(2)}) %collective-permute-start.31) | collective-permute-done | bytes 327712 | tf_op jit(solution)/shard_map/ppermute | solution.py:290
  (76 shorter events, 50.1 us)
Async XLA Ops:
  14.7 61.2 %collective-permute-start.3 = (bf16[4,128,2688]{2,1,0:T(8,128)(2,1)S(1)}, bf16[4,128,2688]{2,1,0:T(8,128)(2,1)S(1)}, u32[]{:S(2)}, u32[]{:S(2)}) collective-permute-start(bf16[4,128,2688]{2,1,0:T(8,128)(2,1)S(1)} %get-tuple-element.62), channel_id=1, source_target_pairs={{0,8},{4,12},{8,0},{12,4},{16,24},{20,28},{24,16},{28,20},{32,40},... | collective-permute-start | bytes 8257544 | tf_op jit(solution)/shard_map/ppermute | solution.py:285
  14.8 12.7 %collective-permute-start.10 = (bf16[128,1280]{1,0:T(8,128)(2,1)S(1)}, bf16[128,1280]{1,0:T(8,128)(2,1)S(1)}, u32[]{:S(2)}, u32[]{:S(2)}) collective-permute-start(bf16[128,1280]{1,0:T(8,128)(2,1)S(1)} %get-tuple-element.63.refs_2_), channel_id=1, source_target_pairs={{0,16},{4,20},{8,24},{12,28},{16,32},{20,36},{24,40},{28,44},{32,4... | collective-permute-start | bytes 983048 | tf_op jit(solution)/shard_map/ppermute | solution.py:298
  19.8 13.6 %collective-permute-start.4 = (bf16[128,1280]{1,0:T(8,128)(2,1)S(1)}, bf16[128,1280]{1,0:T(8,128)(2,1)S(1)}, u32[]{:S(2)}, u32[]{:S(2)}) collective-permute-start(bf16[128,1280]{1,0:T(8,128)(2,1)S(1)} %get-tuple-element.63.refs_2_), channel_id=1, source_target_pairs={{0,112},{4,116},{8,120},{12,124},{16,0},{20,4},{24,8},{28,12},{32,... | collective-permute-start | bytes 983048 | tf_op jit(solution)/shard_map/ppermute | solution.py:298
  21.3 15.6 %collective-permute-start.15 = (bf16[128,1280]{1,0:T(8,128)(2,1)S(1)}, bf16[128,1280]{1,0:T(8,128)(2,1)S(1)}, u32[]{:S(2)}, u32[]{:S(2)}) collective-permute-start(bf16[128,1280]{1,0:T(8,128)(2,1)S(1)} %get-tuple-element.61.refs_3_), channel_id=1, source_target_pairs={{0,16},{4,20},{8,24},{12,28},{16,32},{20,36},{24,40},{28,44},{32,4... | collective-permute-start | bytes 983048 | tf_op jit(solution)/shard_map/ppermute | solution.py:298
  27.4 14.0 %collective-permute-start.11 = (bf16[128,1280]{1,0:T(8,128)(2,1)S(1)}, bf16[128,1280]{1,0:T(8,128)(2,1)S(1)}, u32[]{:S(2)}, u32[]{:S(2)}) collective-permute-start(bf16[128,1280]{1,0:T(8,128)(2,1)S(1)} %collective-permute-done.10.refs_16_), channel_id=1, source_target_pairs={{0,16},{4,20},{8,24},{12,28},{16,32},{20,36},{24,40},{28,44},{32,4... | collective-permute-start | bytes 983048 | tf_op jit(solution)/shard_map/ppermute | solution.py:298
  27.5 14.0 %collective-permute-start.7 = (bf16[128,1280]{1,0:T(8,128)(2,1)S(1)}, bf16[128,1280]{1,0:T(8,128)(2,1)S(1)}, u32[]{:S(2)}, u32[]{:S(2)}) collective-permute-start(bf16[128,1280]{1,0:T(8,128)(2,1)S(1)} %collective-permute-done.5.refs_5_), channel_id=1, source_target_pairs={{0,112},{4,116},{8,120},{12,124},{16,0},{20,4},{24,8},{28,12},{32,... | collective-permute-start | bytes 983048 | tf_op jit(solution)/shard_map/ppermute | solution.py:298
  33.4 14.0 %collective-permute-start.6 = (bf16[128,1280]{1,0:T(8,128)(2,1)S(1)}, bf16[128,1280]{1,0:T(8,128)(2,1)S(1)}, u32[]{:S(2)}, u32[]{:S(2)}) collective-permute-start(bf16[128,1280]{1,0:T(8,128)(2,1)S(1)} %collective-permute-done.4.refs_4_), channel_id=1, source_target_pairs={{0,112},{4,116},{8,120},{12,124},{16,0},{20,4},{24,8},{28,12},{32,... | collective-permute-start | bytes 983048 | tf_op jit(solution)/shard_map/ppermute | solution.py:298
  36.8 14.0 %collective-permute-start.16 = (bf16[128,1280]{1,0:T(8,128)(2,1)S(1)}, bf16[128,1280]{1,0:T(8,128)(2,1)S(1)}, u32[]{:S(2)}, u32[]{:S(2)}) collective-permute-start(bf16[128,1280]{1,0:T(8,128)(2,1)S(1)} %collective-permute-done.15.refs_17_), channel_id=1, source_target_pairs={{0,16},{4,20},{8,24},{12,28},{16,32},{20,36},{24,40},{28,44},{32,4... | collective-permute-start | bytes 983048 | tf_op jit(solution)/shard_map/ppermute | solution.py:298
  41.5 12.9 %collective-permute-start.12 = (bf16[128,1280]{1,0:T(8,128)(2,1)S(1)}, bf16[128,1280]{1,0:T(8,128)(2,1)S(1)}, u32[]{:S(2)}, u32[]{:S(2)}) collective-permute-start(bf16[128,1280]{1,0:T(8,128)(2,1)S(1)} %collective-permute-done.11.refs_14_), channel_id=1, source_target_pairs={{0,16},{4,20},{8,24},{12,28},{16,32},{20,36},{24,40},{28,44},{32,4... | collective-permute-start | bytes 983048 | tf_op jit(solution)/shard_map/ppermute | solution.py:298
  41.5 13.0 %collective-permute-start.9 = (bf16[128,1280]{1,0:T(8,128)(2,1)S(1)}, bf16[128,1280]{1,0:T(8,128)(2,1)S(1)}, u32[]{:S(2)}, u32[]{:S(2)}) collective-permute-start(bf16[128,1280]{1,0:T(8,128)(2,1)S(1)} %collective-permute-done.7.refs_7_), channel_id=1, source_target_pairs={{0,112},{4,116},{8,120},{12,124},{16,0},{20,4},{24,8},{28,12},{32,... | collective-permute-start | bytes 983048 | tf_op jit(solution)/shard_map/ppermute | solution.py:298
  47.5 14.0 %collective-permute-start.8 = (bf16[128,1280]{1,0:T(8,128)(2,1)S(1)}, bf16[128,1280]{1,0:T(8,128)(2,1)S(1)}, u32[]{:S(2)}, u32[]{:S(2)}) collective-permute-start(bf16[128,1280]{1,0:T(8,128)(2,1)S(1)} %collective-permute-done.6.refs_6_), channel_id=1, source_target_pairs={{0,112},{4,116},{8,120},{12,124},{16,0},{20,4},{24,8},{28,12},{32,... | collective-permute-start | bytes 983048 | tf_op jit(solution)/shard_map/ppermute | solution.py:298
  50.9 12.9 %collective-permute-start.17 = (bf16[128,1280]{1,0:T(8,128)(2,1)S(1)}, bf16[128,1280]{1,0:T(8,128)(2,1)S(1)}, u32[]{:S(2)}, u32[]{:S(2)}) collective-permute-start(bf16[128,1280]{1,0:T(8,128)(2,1)S(1)} %collective-permute-done.16.refs_15_), channel_id=1, source_target_pairs={{0,16},{4,20},{8,24},{12,28},{16,32},{20,36},{24,40},{28,44},{32,4... | collective-permute-start | bytes 983048 | tf_op jit(solution)/shard_map/ppermute | solution.py:298
  54.4 14.0 %collective-permute-start.13 = (bf16[128,1280]{1,0:T(8,128)(2,1)S(1)}, bf16[128,1280]{1,0:T(8,128)(2,1)S(1)}, u32[]{:S(2)}, u32[]{:S(2)}) collective-permute-start(bf16[128,1280]{1,0:T(8,128)(2,1)S(1)} %collective-permute-done.12.refs_12_), channel_id=1, source_target_pairs={{0,16},{4,20},{8,24},{12,28},{16,32},{20,36},{24,40},{28,44},{32,4... | collective-permute-start | bytes 983048 | tf_op jit(solution)/shard_map/ppermute | solution.py:298
  54.5 14.0 %collective-permute-start.14 = (bf16[128,1280]{1,0:T(8,128)(2,1)S(1)}, bf16[128,1280]{1,0:T(8,128)(2,1)S(1)}, u32[]{:S(2)}, u32[]{:S(2)}) collective-permute-start(bf16[128,1280]{1,0:T(8,128)(2,1)S(1)} %collective-permute-done.9.refs_9_), channel_id=1, source_target_pairs={{0,112},{4,116},{8,120},{12,124},{16,0},{20,4},{24,8},{28,12},{32,... | collective-permute-start | bytes 983048 | tf_op jit(solution)/shard_map/ppermute | solution.py:298
  61.5 18.6 %collective-permute-start.22 = (bf16[4,128,2688]{2,1,0:T(8,128)(2,1)S(1)}, bf16[4,128,2688]{2,1,0:T(8,128)(2,1)S(1)}, u32[]{:S(2)}, u32[]{:S(2)}) collective-permute-start(bf16[4,128,2688]{2,1,0:T(8,128)(2,1)S(1)} %get-tuple-element.69.refs_1_), channel_id=1, source_target_pairs={{0,4},{4,0},{8,12},{12,8},{16,20},{20,16},{24,28},{28,24},{32,36},... | collective-permute-start | bytes 8257544 | tf_op jit(solution)/shard_map/ppermute | solution.py:285
  75.8 22.4 %collective-permute-start.18 = (bf16[4,128,2688]{2,1,0:T(8,128)(2,1)S(1)}, bf16[4,128,2688]{2,1,0:T(8,128)(2,1)S(1)}, u32[]{:S(2)}, u32[]{:S(2)}) collective-permute-start(bf16[4,128,2688]{2,1,0:T(8,128)(2,1)S(1)} %collective-permute-done.3.refs_0_), channel_id=1, source_target_pairs={{0,4},{4,0},{8,12},{12,8},{16,20},{20,16},{24,28},{28,24},{32,36},... | collective-permute-start | bytes 8257544 | tf_op jit(solution)/shard_map/ppermute | solution.py:285
  78.0 17.1 %collective-permute-start.19 = (bf16[144,1280]{1,0:T(8,128)(2,1)S(1)}, bf16[144,1280]{1,0:T(8,128)(2,1)S(1)}, u32[]{:S(2)}, u32[]{:S(2)}) collective-permute-start(bf16[144,1280]{1,0:T(8,128)(2,1)S(1)} %get-tuple-element.66), channel_id=1, source_target_pairs={{0,1},{1,0},{2,3},{3,2},{4,5},{5,4},{6,7},{7,6},{8,9},{9,8},{10,11... | collective-permute-start | bytes 1105928 | tf_op jit(solution)/shard_map/ppermute | solution.py:294
  78.4 18.3 %collective-permute-start.21 = (bf16[144,1280]{1,0:T(8,128)(2,1)S(1)}, bf16[144,1280]{1,0:T(8,128)(2,1)S(1)}, u32[]{:S(2)}, u32[]{:S(2)}) collective-permute-start(bf16[144,1280]{1,0:T(8,128)(2,1)S(1)} %get-tuple-element.68), channel_id=1, source_target_pairs={{0,3},{1,2},{2,1},{3,0},{4,7},{5,6},{6,5},{7,4},{8,11},{9,10},{10,... | collective-permute-start | bytes 1105928 | tf_op jit(solution)/shard_map/ppermute | solution.py:294
  84.1 25.0 %collective-permute-start.24 = (bf16[2,128,1280]{2,1,0:T(8,128)(2,1)S(1)}, bf16[2,128,1280]{2,1,0:T(8,128)(2,1)S(1)}, u32[]{:S(2)}, u32[]{:S(2)}) collective-permute-start(bf16[2,128,1280]{2,1,0:T(8,128)(2,1)S(1)} %get-tuple-element.81), channel_id=1, source_target_pairs={{0,1},{1,0},{2,3},{3,2},{4,5},{5,4},{6,7},{7,6},{8,9},{9,8},{10,11... | collective-permute-start | bytes 1966088 | tf_op jit(solution)/shard_map/ppermute | solution.py:294
  96.8 17.0 %collective-permute-start.26 = (bf16[2,128,1280]{2,1,0:T(8,128)(2,1)S(1)}, bf16[2,128,1280]{2,1,0:T(8,128)(2,1)S(1)}, u32[]{:S(2)}, u32[]{:S(2)}) collective-permute-start(bf16[2,128,1280]{2,1,0:T(8,128)(2,1)S(1)} %get-tuple-element.85), channel_id=1, source_target_pairs={{0,3},{1,2},{2,1},{3,0},{4,7},{5,6},{6,5},{7,4},{8,11},{9,10},{10,... | collective-permute-start | bytes 1966088 | tf_op jit(solution)/shard_map/ppermute | solution.py:294
  102.3 21.5 %collective-permute-start.23 = (bf16[2,128,1280]{2,1,0:T(8,128)(2,1)S(1)}, bf16[2,128,1280]{2,1,0:T(8,128)(2,1)S(1)}, u32[]{:S(2)}, u32[]{:S(2)}) collective-permute-start(bf16[2,128,1280]{2,1,0:T(8,128)(2,1)S(1)} %get-tuple-element.80), channel_id=1, source_target_pairs={{0,1},{1,0},{2,3},{3,2},{4,5},{5,4},{6,7},{7,6},{8,9},{9,8},{10,11... | collective-permute-start | bytes 1966088 | tf_op jit(solution)/shard_map/ppermute | solution.py:294
  114.0 16.2 %collective-permute-start.29 = (bf16[128,1280]{1,0:T(8,128)(2,1)S(1)}, bf16[128,1280]{1,0:T(8,128)(2,1)S(1)}, u32[]{:S(2)}, u32[]{:S(2)}) collective-permute-start(bf16[128,1280]{1,0:T(8,128)(2,1)S(1)} %get-tuple-element.87), channel_id=1, source_target_pairs={{0,1},{1,0},{2,3},{3,2},{4,5},{5,4},{6,7},{7,6},{8,9},{9,8},{10,11... | collective-permute-start | bytes 983048 | tf_op jit(solution)/shard_map/ppermute | solution.py:294
  121.1 12.0 %collective-permute-start.30 = (bf16[128,1280]{1,0:T(8,128)(2,1)S(1)}, bf16[128,1280]{1,0:T(8,128)(2,1)S(1)}, u32[]{:S(2)}, u32[]{:S(2)}) collective-permute-start(bf16[128,1280]{1,0:T(8,128)(2,1)S(1)} %shard_map.74), channel_id=1, source_target_pairs={{0,132},{4,128},{8,140},{12,136},{16,148},{20,144},{24,156},{28,15... | collective-permute-start | bytes 983048 | tf_op jit(solution)/shard_map/ppermute | solution.py:290
  134.2 14.0 %collective-permute-start.31 = (bf16[128,1280]{1,0:T(8,128)(2,1)S(1)}, bf16[128,1280]{1,0:T(8,128)(2,1)S(1)}, u32[]{:S(2)}, u32[]{:S(2)}) collective-permute-start(bf16[128,1280]{1,0:T(8,128)(2,1)S(1)} %shard_map.77), channel_id=1, source_target_pairs={{0,140},{4,136},{8,132},{12,128},{16,156},{20,152},{24,148},{28,14... | collective-permute-start | bytes 983048 | tf_op jit(solution)/shard_map/ppermute | solution.py:290
  (13 other events, 113.3 us)

commit v3 on v2

--- a/solution.py
+++ b/solution.py
@@ -21,7 +21,7 @@
 CONFIG = {'kinds': (2, 0, 1, 0), 'order': ('P0', 'P1', 'P2', 'T0', 'P3', 'M1', 'M2', 'T1', 'M3', 'T2', 'T3'), 'crossed': ((0, 'T1'), (1, 'T3')), 'far': 'P0', 'hold': {}, 'sends': (2, 1, 3)}
 MORE = 16
 BOTH = 2 * WIDE
-VMEM_LIMIT = 20 * 1024 * 1024
+VMEM_LIMIT = 12 * 1024 * 1024
 MIB = 1024 * 1024
 
 

time: 150 us -> 150 us (level)
  no operation moved by 1% of the time
where the time goes in v3:
time: 150 us
  waiting for transfers between devices  66.7 us (44%)
  starting transfers between devices  51.1 us (34%)
  Pallas kernels  25.2 us (17%)
  local copies, waits for them, and re-layouts  5.05 us (3%)
  other arithmetic  1.6 us (1%)
    ppermute x14, waiting for transfers between devices, along_z(): lax.ppermute(value, 'dp', [(i, (i + steps * GROUP) % DP) for i in range(D...  29.4 us
    ppermute x9, waiting for transfers between devices, along_y(): return lax.ppermute(value, 'tensor', [(i, i ^ offset) for i in range(N_T)])  26.2 us
    ppermute x14, starting transfers between devices, along_z(): lax.ppermute(value, 'dp', [(i, (i + steps * GROUP) % DP) for i in range(D...  22.1 us
    pallas_call x3, Pallas kernels, product(): local(functools.partial(product_body, kind, False), parts_of(kind, TILE),...  12 us
    ppermute x4, starting transfers between devices, cross(): return lax.ppermute(value, ('section', 'dp'), pairs)  11.5 us
    ppermute x9, starting transfers between devices, along_y(): return lax.ppermute(value, 'tensor', [(i, i ^ offset) for i in range(N_T)])  9.06 us
    ppermute x6, starting transfers between devices, swap(): return lax.ppermute(value, 'dp', [(i, i ^ offset) for i in range(DP)])  8.45 us
    ppermute x4, waiting for transfers between devices, cross(): return lax.ppermute(value, ('section', 'dp'), pairs)  7.23 us
  transfers between devices with their start and end apart: 33, of which 19 were waited for; matrix products, arithmetic and copies ran while one was open for 2% of the time, Pallas kernels for 15%

profile of v3, /device:TPU:1, one launch (start us, length us, event | category | flops | bytes accessed | tf_op | source)
XLA Modules:
  0.0 150.1 jit_solution(12164762521156978130)
XLA Ops:
  1.3 3.3 %collective-permute-start = (bf16[64,1280]{1,0:T(8,128)(2,1)S(1)}, bf16[64,1280]{1,0:T(8,128)(2,1)S(1)}, u32[]{:S(2)}, u32[]{:S(2)}) collective-permute-start(bf16[64,1280]{1,0:T(8,128)(2,1)S(1)} %get-tuple-element.54), channel_id=1, source_target_pairs={{0,4},{4,0},{8,12},{12,8},{16,20},{20,16},{24,28},{28,24},{32,36},... | collective-permute-start | bytes 491528 | tf_op jit(solution)/shard_map/ppermute | solution.py:285
  15.9 3.9 %collective-permute-start.5 = (bf16[128,1280]{1,0:T(8,128)(2,1)S(1)}, bf16[128,1280]{1,0:T(8,128)(2,1)S(1)}, u32[]{:S(2)}, u32[]{:S(2)}) collective-permute-start(bf16[128,1280]{1,0:T(8,128)(2,1)S(1)} %get-tuple-element.61.refs_3_), channel_id=1, source_target_pairs={{0,112},{4,116},{8,120},{12,124},{16,0},{20,4},{24,8},{28,12},{32,... | collective-permute-start | bytes 983048 | tf_op jit(solution)/shard_map/ppermute | solution.py:298
  21.3 6.2 %collective-permute-done.10.refs_16_ = bf16[128,1280]{1,0:T(8,128)(2,1)S(1)} collective-permute-done((bf16[128,1280]{1,0:T(8,128)(2,1)S(1)}, bf16[128,1280]{1,0:T(8,128)(2,1)S(1)}, u32[]{:S(2)}, u32[]{:S(2)}) %collective-permute-start.10) | collective-permute-done | bytes 327712 | tf_op jit(solution)/shard_map/ppermute | solution.py:298
  30.1 3.3 %collective-permute-done.4.refs_4_ = bf16[128,1280]{1,0:T(8,128)(2,1)S(1)} collective-permute-done((bf16[128,1280]{1,0:T(8,128)(2,1)S(1)}, bf16[128,1280]{1,0:T(8,128)(2,1)S(1)}, u32[]{:S(2)}, u32[]{:S(2)}) %collective-permute-start.4) | collective-permute-done | bytes 327712 | tf_op jit(solution)/shard_map/ppermute | solution.py:298
  33.4 3.4 %collective-permute-start.6 = (bf16[128,1280]{1,0:T(8,128)(2,1)S(1)}, bf16[128,1280]{1,0:T(8,128)(2,1)S(1)}, u32[]{:S(2)}, u32[]{:S(2)}) collective-permute-start(bf16[128,1280]{1,0:T(8,128)(2,1)S(1)} %collective-permute-done.4.refs_4_), channel_id=1, source_target_pairs={{0,112},{4,116},{8,120},{12,124},{16,0},{20,4},{24,8},{28,12},{32,... | collective-permute-start | bytes 983048 | tf_op jit(solution)/shard_map/ppermute | solution.py:298
  36.8 4.7 %collective-permute-done.11.refs_14_ = bf16[128,1280]{1,0:T(8,128)(2,1)S(1)} collective-permute-done((bf16[128,1280]{1,0:T(8,128)(2,1)S(1)}, bf16[128,1280]{1,0:T(8,128)(2,1)S(1)}, u32[]{:S(2)}, u32[]{:S(2)}) %collective-permute-start.11) | collective-permute-done | bytes 327712 | tf_op jit(solution)/shard_map/ppermute | solution.py:298
  44.2 3.3 %collective-permute-done.6.refs_6_ = bf16[128,1280]{1,0:T(8,128)(2,1)S(1)} collective-permute-done((bf16[128,1280]{1,0:T(8,128)(2,1)S(1)}, bf16[128,1280]{1,0:T(8,128)(2,1)S(1)}, u32[]{:S(2)}, u32[]{:S(2)}) %collective-permute-start.6) | collective-permute-done | bytes 327712 | tf_op jit(solution)/shard_map/ppermute | solution.py:298
  47.5 3.4 %collective-permute-start.8 = (bf16[128,1280]{1,0:T(8,128)(2,1)S(1)}, bf16[128,1280]{1,0:T(8,128)(2,1)S(1)}, u32[]{:S(2)}, u32[]{:S(2)}) collective-permute-start(bf16[128,1280]{1,0:T(8,128)(2,1)S(1)} %collective-permute-done.6.refs_6_), channel_id=1, source_target_pairs={{0,112},{4,116},{8,120},{12,124},{16,0},{20,4},{24,8},{28,12},{32,... | collective-permute-start | bytes 983048 | tf_op jit(solution)/shard_map/ppermute | solution.py:298
  50.9 3.6 %collective-permute-done.12.refs_12_ = bf16[128,1280]{1,0:T(8,128)(2,1)S(1)} collective-permute-done((bf16[128,1280]{1,0:T(8,128)(2,1)S(1)}, bf16[128,1280]{1,0:T(8,128)(2,1)S(1)}, u32[]{:S(2)}, u32[]{:S(2)}) %collective-permute-start.12) | collective-permute-done | bytes 327712 | tf_op jit(solution)/shard_map/ppermute | solution.py:298
  54.5 3.4 %collective-permute-start.14 = (bf16[128,1280]{1,0:T(8,128)(2,1)S(1)}, bf16[128,1280]{1,0:T(8,128)(2,1)S(1)}, u32[]{:S(2)}, u32[]{:S(2)}) collective-permute-start(bf16[128,1280]{1,0:T(8,128)(2,1)S(1)} %collective-permute-done.9.refs_9_), channel_id=1, source_target_pairs={{0,112},{4,116},{8,120},{12,124},{16,0},{20,4},{24,8},{28,12},{32,... | collective-permute-start | bytes 983048 | tf_op jit(solution)/shard_map/ppermute | solution.py:298
  57.9 3.6 %collective-permute-done.8.refs_8_ = bf16[128,1280]{1,0:T(8,128)(2,1)S(1)} collective-permute-done((bf16[128,1280]{1,0:T(8,128)(2,1)S(1)}, bf16[128,1280]{1,0:T(8,128)(2,1)S(1)}, u32[]{:S(2)}, u32[]{:S(2)}) %collective-permute-start.8) | collective-permute-done | bytes 327712 | tf_op jit(solution)/shard_map/ppermute | solution.py:298
  63.8 4.7 %collective-permute-done.13.refs_10_ = bf16[128,1280]{1,0:T(8,128)(2,1)S(1)} collective-permute-done((bf16[128,1280]{1,0:T(8,128)(2,1)S(1)}, bf16[128,1280]{1,0:T(8,128)(2,1)S(1)}, u32[]{:S(2)}, u32[]{:S(2)}) %collective-permute-start.13) | collective-permute-done | bytes 327712 | tf_op jit(solution)/shard_map/ppermute | solution.py:298
  68.5 4.3 %shard_map.67 = (bf16[144,1280]{1,0:T(8,128)(2,1)S(1)}, bf16[144,1280]{1,0:T(8,128)(2,1)S(1)}, bf16[144,1280]{1,0:T(8,128)(2,1)S(1)}, bf16[144,1280]{1,0:T(8,128)(2,1)S(1)}, bf16[2048,1280]{1,0:T(8,128)(2,1)S(1)}) custom-call(s32[8]{0:T(128)S(1)} %concatenate.3.sc, bf16[4,16,1280]{2,1,0:T(8,128)(2,1)S(1)} %convert_element_type.11.refs_0_, ...), custom_call_target="tpu_custom_call" | custom-call | flops 41943040 | bytes 131072 | tf_op jit(solution)/shard_map/pallas_call | solution.py:197
  72.9 3.0 %collective-permute-done.3.refs_0_ = bf16[4,128,2688]{2,1,0:T(8,128)(2,1)S(1)} collective-permute-done((bf16[4,128,2688]{2,1,0:T(8,128)(2,1)S(1)}, bf16[4,128,2688]{2,1,0:T(8,128)(2,1)S(1)}, u32[]{:S(2)}, u32[]{:S(2)}) %collective-permute-start.3) | collective-permute-done | bytes 2752544 | tf_op jit(solution)/shard_map/ppermute | solution.py:285
  80.1 4.0 %shard_map.68 = (bf16[2,128,1280]{2,1,0:T(8,128)(2,1)S(1)}, bf16[2,128,1280]{2,1,0:T(8,128)(2,1)S(1)}) custom-call(s32[8]{0:T(128)S(1)} %concatenate.3.sc, bf16[4,128,2688]{2,1,0:T(8,128)(2,1)S(1)} %collective-permute-done.22.refs_0_, bf16[2048,1280]{1,0:T(8,128)(2,1)S(1)} %get-tuple-element.71.refs_1_), custom_call_target="tpu_custom_call" | custom-call | flops 41943040 | bytes 131072 | tf_op jit(solution)/shard_map/pallas_call | solution.py:208
  84.4 4.0 %shard_map.69 = (bf16[2,128,1280]{2,1,0:T(8,128)(2,1)S(1)}, bf16[2,128,1280]{2,1,0:T(8,128)(2,1)S(1)}) custom-call(s32[8]{0:T(128)S(1)} %concatenate.3.sc, bf16[4,128,2688]{2,1,0:T(8,128)(2,1)S(1)} %collective-permute-done.3.refs_0_, bf16[2048,1280]{1,0:T(8,128)(2,1)S(1)} %get-tuple-element.71.refs_1_), custom_call_target="tpu_custom_call" | custom-call | flops 41943040 | bytes 131072 | tf_op jit(solution)/shard_map/pallas_call | solution.py:208
  88.6 6.5 %collective-permute-done.19.refs_1_ = bf16[144,1280]{1,0:T(8,128)(2,1)S(1)} collective-permute-done((bf16[144,1280]{1,0:T(8,128)(2,1)S(1)}, bf16[144,1280]{1,0:T(8,128)(2,1)S(1)}, u32[]{:S(2)}, u32[]{:S(2)}) %collective-permute-start.19) | collective-permute-done | bytes 368672 | tf_op jit(solution)/shard_map/ppermute | solution.py:294
  98.3 4.0 %shard_map.71 = (bf16[2,128,1280]{2,1,0:T(8,128)(2,1)S(1)}, bf16[2,128,1280]{2,1,0:T(8,128)(2,1)S(1)}) custom-call(s32[8]{0:T(128)S(1)} %concatenate.3.sc, bf16[4,128,2688]{2,1,0:T(8,128)(2,1)S(1)} %collective-permute-done.18.refs_0_, bf16[2048,1280]{1,0:T(8,128)(2,1)S(1)} %get-tuple-element.71.refs_1_), custom_call_target="tpu_custom_call" | custom-call | flops 41943040 | bytes 131072 | tf_op jit(solution)/shard_map/pallas_call | solution.py:208
  102.4 2.9 %collective-permute-start.27 = (bf16[144,1280]{1,0:T(8,128)(2,1)S(1)}, bf16[144,1280]{1,0:T(8,128)(2,1)S(1)}, u32[]{:S(2)}, u32[]{:S(2)}) collective-permute-start(bf16[144,1280]{1,0:T(8,128)(2,1)S(1)} %shard_map.70), channel_id=1, source_target_pairs={{0,128},{4,132},{8,136},{12,140},{16,144},{20,148},{24,152},{28,15... | collective-permute-start | bytes 1105928 | tf_op jit(solution)/shard_map/ppermute | solution.py:290
  105.2 3.9 %collective-permute-done.24.b_ref = bf16[2,128,1280]{2,1,0:T(8,128)(2,1)S(1)} collective-permute-done((bf16[2,128,1280]{2,1,0:T(8,128)(2,1)S(1)}, bf16[2,128,1280]{2,1,0:T(8,128)(2,1)S(1)}, u32[]{:S(2)}, u32[]{:S(2)}) %collective-permute-start.24) | collective-permute-done | bytes 655392 | tf_op jit(solution)/shard_map/ppermute | solution.py:294
  114.1 6.7 %collective-permute-done.25.refs_1_ = bf16[128,1280]{1,0:T(8,128)(2,1)S(1)} collective-permute-done((bf16[128,1280]{1,0:T(8,128)(2,1)S(1)}, bf16[128,1280]{1,0:T(8,128)(2,1)S(1)}, u32[]{:S(2)}, u32[]{:S(2)}) %collective-permute-start.25) | collective-permute-done | bytes 327712 | tf_op jit(solution)/shard_map/ppermute | solution.py:294
  126.5 3.7 %collective-permute-done.29.refs_1_ = bf16[128,1280]{1,0:T(8,128)(2,1)S(1)} collective-permute-done((bf16[128,1280]{1,0:T(8,128)(2,1)S(1)}, bf16[128,1280]{1,0:T(8,128)(2,1)S(1)}, u32[]{:S(2)}, u32[]{:S(2)}) %collective-permute-start.29) | collective-permute-done | bytes 327712 | tf_op jit(solution)/shard_map/ppermute | solution.py:294
  134.2 3.3 %collective-permute-start.31 = (bf16[128,1280]{1,0:T(8,128)(2,1)S(1)}, bf16[128,1280]{1,0:T(8,128)(2,1)S(1)}, u32[]{:S(2)}, u32[]{:S(2)}) collective-permute-start(bf16[128,1280]{1,0:T(8,128)(2,1)S(1)} %shard_map.77), channel_id=1, source_target_pairs={{0,140},{4,136},{8,132},{12,128},{16,156},{20,152},{24,148},{28,14... | collective-permute-start | bytes 983048 | tf_op jit(solution)/shard_map/ppermute | solution.py:290
  141.8 6.5 %collective-permute-done.31.refs_0_ = bf16[128,1280]{1,0:T(8,128)(2,1)S(1)} collective-permute-done((bf16[128,1280]{1,0:T(8,128)(2,1)S(1)}, bf16[128,1280]{1,0:T(8,128)(2,1)S(1)}, u32[]{:S(2)}, u32[]{:S(2)}) %collective-permute-start.31) | collective-permute-done | bytes 327712 | tf_op jit(solution)/shard_map/ppermute | solution.py:290
  (76 shorter events, 50.1 us)
Async XLA Ops:
  14.7 61.2 %collective-permute-start.3 = (bf16[4,128,2688]{2,1,0:T(8,128)(2,1)S(1)}, bf16[4,128,2688]{2,1,0:T(8,128)(2,1)S(1)}, u32[]{:S(2)}, u32[]{:S(2)}) collective-permute-start(bf16[4,128,2688]{2,1,0:T(8,128)(2,1)S(1)} %get-tuple-element.62), channel_id=1, source_target_pairs={{0,8},{4,12},{8,0},{12,4},{16,24},{20,28},{24,16},{28,20},{32,40},... | collective-permute-start | bytes 8257544 | tf_op jit(solution)/shard_map/ppermute | solution.py:285
  14.8 12.7 %collective-permute-start.10 = (bf16[128,1280]{1,0:T(8,128)(2,1)S(1)}, bf16[128,1280]{1,0:T(8,128)(2,1)S(1)}, u32[]{:S(2)}, u32[]{:S(2)}) collective-permute-start(bf16[128,1280]{1,0:T(8,128)(2,1)S(1)} %get-tuple-element.63.refs_2_), channel_id=1, source_target_pairs={{0,16},{4,20},{8,24},{12,28},{16,32},{20,36},{24,40},{28,44},{32,4... | collective-permute-start | bytes 983048 | tf_op jit(solution)/shard_map/ppermute | solution.py:298
  19.8 13.6 %collective-permute-start.4 = (bf16[128,1280]{1,0:T(8,128)(2,1)S(1)}, bf16[128,1280]{1,0:T(8,128)(2,1)S(1)}, u32[]{:S(2)}, u32[]{:S(2)}) collective-permute-start(bf16[128,1280]{1,0:T(8,128)(2,1)S(1)} %get-tuple-element.63.refs_2_), channel_id=1, source_target_pairs={{0,112},{4,116},{8,120},{12,124},{16,0},{20,4},{24,8},{28,12},{32,... | collective-permute-start | bytes 983048 | tf_op jit(solution)/shard_map/ppermute | solution.py:298
  21.3 15.6 %collective-permute-start.15 = (bf16[128,1280]{1,0:T(8,128)(2,1)S(1)}, bf16[128,1280]{1,0:T(8,128)(2,1)S(1)}, u32[]{:S(2)}, u32[]{:S(2)}) collective-permute-start(bf16[128,1280]{1,0:T(8,128)(2,1)S(1)} %get-tuple-element.61.refs_3_), channel_id=1, source_target_pairs={{0,16},{4,20},{8,24},{12,28},{16,32},{20,36},{24,40},{28,44},{32,4... | collective-permute-start | bytes 983048 | tf_op jit(solution)/shard_map/ppermute | solution.py:298
  27.4 14.0 %collective-permute-start.11 = (bf16[128,1280]{1,0:T(8,128)(2,1)S(1)}, bf16[128,1280]{1,0:T(8,128)(2,1)S(1)}, u32[]{:S(2)}, u32[]{:S(2)}) collective-permute-start(bf16[128,1280]{1,0:T(8,128)(2,1)S(1)} %collective-permute-done.10.refs_16_), channel_id=1, source_target_pairs={{0,16},{4,20},{8,24},{12,28},{16,32},{20,36},{24,40},{28,44},{32,4... | collective-permute-start | bytes 983048 | tf_op jit(solution)/shard_map/ppermute | solution.py:298
  27.5 14.0 %collective-permute-start.7 = (bf16[128,1280]{1,0:T(8,128)(2,1)S(1)}, bf16[128,1280]{1,0:T(8,128)(2,1)S(1)}, u32[]{:S(2)}, u32[]{:S(2)}) collective-permute-start(bf16[128,1280]{1,0:T(8,128)(2,1)S(1)} %collective-permute-done.5.refs_5_), channel_id=1, source_target_pairs={{0,112},{4,116},{8,120},{12,124},{16,0},{20,4},{24,8},{28,12},{32,... | collective-permute-start | bytes 983048 | tf_op jit(solution)/shard_map/ppermute | solution.py:298
  33.4 14.0 %collective-permute-start.6 = (bf16[128,1280]{1,0:T(8,128)(2,1)S(1)}, bf16[128,1280]{1,0:T(8,128)(2,1)S(1)}, u32[]{:S(2)}, u32[]{:S(2)}) collective-permute-start(bf16[128,1280]{1,0:T(8,128)(2,1)S(1)} %collective-permute-done.4.refs_4_), channel_id=1, source_target_pairs={{0,112},{4,116},{8,120},{12,124},{16,0},{20,4},{24,8},{28,12},{32,... | collective-permute-start | bytes 983048 | tf_op jit(solution)/shard_map/ppermute | solution.py:298
  36.8 14.0 %collective-permute-start.16 = (bf16[128,1280]{1,0:T(8,128)(2,1)S(1)}, bf16[128,1280]{1,0:T(8,128)(2,1)S(1)}, u32[]{:S(2)}, u32[]{:S(2)}) collective-permute-start(bf16[128,1280]{1,0:T(8,128)(2,1)S(1)} %collective-permute-done.15.refs_17_), channel_id=1, source_target_pairs={{0,16},{4,20},{8,24},{12,28},{16,32},{20,36},{24,40},{28,44},{32,4... | collective-permute-start | bytes 983048 | tf_op jit(solution)/shard_map/ppermute | solution.py:298
  41.5 12.9 %collective-permute-start.12 = (bf16[128,1280]{1,0:T(8,128)(2,1)S(1)}, bf16[128,1280]{1,0:T(8,128)(2,1)S(1)}, u32[]{:S(2)}, u32[]{:S(2)}) collective-permute-start(bf16[128,1280]{1,0:T(8,128)(2,1)S(1)} %collective-permute-done.11.refs_14_), channel_id=1, source_target_pairs={{0,16},{4,20},{8,24},{12,28},{16,32},{20,36},{24,40},{28,44},{32,4... | collective-permute-start | bytes 983048 | tf_op jit(solution)/shard_map/ppermute | solution.py:298
  41.5 13.0 %collective-permute-start.9 = (bf16[128,1280]{1,0:T(8,128)(2,1)S(1)}, bf16[128,1280]{1,0:T(8,128)(2,1)S(1)}, u32[]{:S(2)}, u32[]{:S(2)}) collective-permute-start(bf16[128,1280]{1,0:T(8,128)(2,1)S(1)} %collective-permute-done.7.refs_7_), channel_id=1, source_target_pairs={{0,112},{4,116},{8,120},{12,124},{16,0},{20,4},{24,8},{28,12},{32,... | collective-permute-start | bytes 983048 | tf_op jit(solution)/shard_map/ppermute | solution.py:298
  47.5 14.0 %collective-permute-start.8 = (bf16[128,1280]{1,0:T(8,128)(2,1)S(1)}, bf16[128,1280]{1,0:T(8,128)(2,1)S(1)}, u32[]{:S(2)}, u32[]{:S(2)}) collective-permute-start(bf16[128,1280]{1,0:T(8,128)(2,1)S(1)} %collective-permute-done.6.refs_6_), channel_id=1, source_target_pairs={{0,112},{4,116},{8,120},{12,124},{16,0},{20,4},{24,8},{28,12},{32,... | collective-permute-start | bytes 983048 | tf_op jit(solution)/shard_map/ppermute | solution.py:298
  50.9 12.9 %collective-permute-start.17 = (bf16[128,1280]{1,0:T(8,128)(2,1)S(1)}, bf16[128,1280]{1,0:T(8,128)(2,1)S(1)}, u32[]{:S(2)}, u32[]{:S(2)}) collective-permute-start(bf16[128,1280]{1,0:T(8,128)(2,1)S(1)} %collective-permute-done.16.refs_15_), channel_id=1, source_target_pairs={{0,16},{4,20},{8,24},{12,28},{16,32},{20,36},{24,40},{28,44},{32,4... | collective-permute-start | bytes 983048 | tf_op jit(solution)/shard_map/ppermute | solution.py:298
  54.4 14.0 %collective-permute-start.13 = (bf16[128,1280]{1,0:T(8,128)(2,1)S(1)}, bf16[128,1280]{1,0:T(8,128)(2,1)S(1)}, u32[]{:S(2)}, u32[]{:S(2)}) collective-permute-start(bf16[128,1280]{1,0:T(8,128)(2,1)S(1)} %collective-permute-done.12.refs_12_), channel_id=1, source_target_pairs={{0,16},{4,20},{8,24},{12,28},{16,32},{20,36},{24,40},{28,44},{32,4... | collective-permute-start | bytes 983048 | tf_op jit(solution)/shard_map/ppermute | solution.py:298
  54.5 14.0 %collective-permute-start.14 = (bf16[128,1280]{1,0:T(8,128)(2,1)S(1)}, bf16[128,1280]{1,0:T(8,128)(2,1)S(1)}, u32[]{:S(2)}, u32[]{:S(2)}) collective-permute-start(bf16[128,1280]{1,0:T(8,128)(2,1)S(1)} %collective-permute-done.9.refs_9_), channel_id=1, source_target_pairs={{0,112},{4,116},{8,120},{12,124},{16,0},{20,4},{24,8},{28,12},{32,... | collective-permute-start | bytes 983048 | tf_op jit(solution)/shard_map/ppermute | solution.py:298
  61.5 18.6 %collective-permute-start.22 = (bf16[4,128,2688]{2,1,0:T(8,128)(2,1)S(1)}, bf16[4,128,2688]{2,1,0:T(8,128)(2,1)S(1)}, u32[]{:S(2)}, u32[]{:S(2)}) collective-permute-start(bf16[4,128,2688]{2,1,0:T(8,128)(2,1)S(1)} %get-tuple-element.69.refs_1_), channel_id=1, source_target_pairs={{0,4},{4,0},{8,12},{12,8},{16,20},{20,16},{24,28},{28,24},{32,36},... | collective-permute-start | bytes 8257544 | tf_op jit(solution)/shard_map/ppermute | solution.py:285
  75.8 22.4 %collective-permute-start.18 = (bf16[4,128,2688]{2,1,0:T(8,128)(2,1)S(1)}, bf16[4,128,2688]{2,1,0:T(8,128)(2,1)S(1)}, u32[]{:S(2)}, u32[]{:S(2)}) collective-permute-start(bf16[4,128,2688]{2,1,0:T(8,128)(2,1)S(1)} %collective-permute-done.3.refs_0_), channel_id=1, source_target_pairs={{0,4},{4,0},{8,12},{12,8},{16,20},{20,16},{24,28},{28,24},{32,36},... | collective-permute-start | bytes 8257544 | tf_op jit(solution)/shard_map/ppermute | solution.py:285
  78.0 17.1 %collective-permute-start.19 = (bf16[144,1280]{1,0:T(8,128)(2,1)S(1)}, bf16[144,1280]{1,0:T(8,128)(2,1)S(1)}, u32[]{:S(2)}, u32[]{:S(2)}) collective-permute-start(bf16[144,1280]{1,0:T(8,128)(2,1)S(1)} %get-tuple-element.66), channel_id=1, source_target_pairs={{0,1},{1,0},{2,3},{3,2},{4,5},{5,4},{6,7},{7,6},{8,9},{9,8},{10,11... | collective-permute-start | bytes 1105928 | tf_op jit(solution)/shard_map/ppermute | solution.py:294
  78.4 18.3 %collective-permute-start.21 = (bf16[144,1280]{1,0:T(8,128)(2,1)S(1)}, bf16[144,1280]{1,0:T(8,128)(2,1)S(1)}, u32[]{:S(2)}, u32[]{:S(2)}) collective-permute-start(bf16[144,1280]{1,0:T(8,128)(2,1)S(1)} %get-tuple-element.68), channel_id=1, source_target_pairs={{0,3},{1,2},{2,1},{3,0},{4,7},{5,6},{6,5},{7,4},{8,11},{9,10},{10,... | collective-permute-start | bytes 1105928 | tf_op jit(solution)/shard_map/ppermute | solution.py:294
  84.1 25.0 %collective-permute-start.24 = (bf16[2,128,1280]{2,1,0:T(8,128)(2,1)S(1)}, bf16[2,128,1280]{2,1,0:T(8,128)(2,1)S(1)}, u32[]{:S(2)}, u32[]{:S(2)}) collective-permute-start(bf16[2,128,1280]{2,1,0:T(8,128)(2,1)S(1)} %get-tuple-element.81), channel_id=1, source_target_pairs={{0,1},{1,0},{2,3},{3,2},{4,5},{5,4},{6,7},{7,6},{8,9},{9,8},{10,11... | collective-permute-start | bytes 1966088 | tf_op jit(solution)/shard_map/ppermute | solution.py:294
  96.8 17.0 %collective-permute-start.26 = (bf16[2,128,1280]{2,1,0:T(8,128)(2,1)S(1)}, bf16[2,128,1280]{2,1,0:T(8,128)(2,1)S(1)}, u32[]{:S(2)}, u32[]{:S(2)}) collective-permute-start(bf16[2,128,1280]{2,1,0:T(8,128)(2,1)S(1)} %get-tuple-element.85), channel_id=1, source_target_pairs={{0,3},{1,2},{2,1},{3,0},{4,7},{5,6},{6,5},{7,4},{8,11},{9,10},{10,... | collective-permute-start | bytes 1966088 | tf_op jit(solution)/shard_map/ppermute | solution.py:294
  102.3 21.5 %collective-permute-start.23 = (bf16[2,128,1280]{2,1,0:T(8,128)(2,1)S(1)}, bf16[2,128,1280]{2,1,0:T(8,128)(2,1)S(1)}, u32[]{:S(2)}, u32[]{:S(2)}) collective-permute-start(bf16[2,128,1280]{2,1,0:T(8,128)(2,1)S(1)} %get-tuple-element.80), channel_id=1, source_target_pairs={{0,1},{1,0},{2,3},{3,2},{4,5},{5,4},{6,7},{7,6},{8,9},{9,8},{10,11... | collective-permute-start | bytes 1966088 | tf_op jit(solution)/shard_map/ppermute | solution.py:294
  114.0 16.2 %collective-permute-start.29 = (bf16[128,1280]{1,0:T(8,128)(2,1)S(1)}, bf16[128,1280]{1,0:T(8,128)(2,1)S(1)}, u32[]{:S(2)}, u32[]{:S(2)}) collective-permute-start(bf16[128,1280]{1,0:T(8,128)(2,1)S(1)} %get-tuple-element.87), channel_id=1, source_target_pairs={{0,1},{1,0},{2,3},{3,2},{4,5},{5,4},{6,7},{7,6},{8,9},{9,8},{10,11... | collective-permute-start | bytes 983048 | tf_op jit(solution)/shard_map/ppermute | solution.py:294
  121.1 12.0 %collective-permute-start.30 = (bf16[128,1280]{1,0:T(8,128)(2,1)S(1)}, bf16[128,1280]{1,0:T(8,128)(2,1)S(1)}, u32[]{:S(2)}, u32[]{:S(2)}) collective-permute-start(bf16[128,1280]{1,0:T(8,128)(2,1)S(1)} %shard_map.74), channel_id=1, source_target_pairs={{0,132},{4,128},{8,140},{12,136},{16,148},{20,144},{24,156},{28,15... | collective-permute-start | bytes 983048 | tf_op jit(solution)/shard_map/ppermute | solution.py:290
  134.2 14.0 %collective-permute-start.31 = (bf16[128,1280]{1,0:T(8,128)(2,1)S(1)}, bf16[128,1280]{1,0:T(8,128)(2,1)S(1)}, u32[]{:S(2)}, u32[]{:S(2)}) collective-permute-start(bf16[128,1280]{1,0:T(8,128)(2,1)S(1)} %shard_map.77), channel_id=1, source_target_pairs={{0,140},{4,136},{8,132},{12,128},{16,156},{20,152},{24,148},{28,14... | collective-permute-start | bytes 983048 | tf_op jit(solution)/shard_map/ppermute | solution.py:290
  (13 other events, 113.3 us)
